TPU v7x, 512 devices: a whole 4x4x16 slice. The times are simulated.
512 devices in a mesh: head: 32 (over x, z_lo), blk: 16 (over z_hi, y, core).
Axes of the slice: x: 4, y: 4, z: 16 (z_hi: 2, z_lo: 8; z = z_hi * 8 + z_lo), core: 2. Of those that a mesh axis runs over, the one named last changes fastest.
Arguments:
- queries: bfloat16 [12288, 4096], P('blk', 'head'), may hold values from -6 to 6
- key_states: bfloat16 [12288, 4096], P('blk', 'head'), may hold values from -6 to 6
- value_states: bfloat16 [12288, 4096], P('blk', 'head'), may hold values from -6 to 6
Outputs:
- attended: bfloat16 [12288, 4096], P(('blk', 'head'))
- heavy_scores: float32 [32, 12288], P('head', 'blk')
All inputs are finite; a program needn't handle non-finite values.
Results may differ from a plain program's by a relative error of at most 0.0085.
Values may be sent and summed in bfloat16 or wider, within the bound.
A program may use at most 64 MiB of HBM per device.

v0:
```python
import math

import jax
import jax.numpy as jnp
from jax import lax
from jax.sharding import PartitionSpec as P

HEAD_DIM = 128


def partner(value, axis, stride):
    mask = 2**stride
    pairs = [(source, source ^ mask) for source in range(lax.axis_size(axis))]
    return lax.ppermute(value, axis, pairs)


def passed_along(value, axis, steps):
    count = lax.axis_size(axis)
    pairs = [(source, (source + steps) % count) for source in range(count)]
    return lax.ppermute(value, axis, pairs)


def local(queries, key_states, value_states):
    scaling = 1.0 / math.sqrt(HEAD_DIM)
    row_count = queries.shape[0]
    half = row_count // 2
    head_count = queries.shape[1] // HEAD_DIM
    block_total = lax.axis_size("blk")
    my_block = lax.axis_index("blk")
    bit_count = block_total.bit_length() - 1
    query_loc = queries.reshape(row_count, head_count, HEAD_DIM)
    key_loc = key_states.reshape(row_count, head_count, HEAD_DIM)
    value_loc = value_states.reshape(row_count, head_count, HEAD_DIM)
    stacked = jnp.stack([query_loc[half:], key_loc[half:], value_loc[half:]])
    for bit in range(bit_count):
        stacked = partner(stacked, "blk", bit)
    query_loc = jnp.concatenate([query_loc[:half], stacked[0]], axis=0)
    key_loc = jnp.concatenate([key_loc[:half], stacked[1]], axis=0)
    value_loc = jnp.concatenate([value_loc[:half], stacked[2]], axis=0)

    def layout_pos(rows):
        shard = rows // row_count
        within = rows % row_count
        return jnp.where(within < half, rows, (block_total - 1 - shard) * row_count + within)

    query_pos = layout_pos(my_block * row_count + jnp.arange(row_count, dtype=jnp.int32))
    query_last = [jnp.max(query_pos[:half]), jnp.max(query_pos[half:])]

    def tile_logits(part_idx, key_tile, key_pos):
        query_rows = query_loc[part_idx * half : (part_idx + 1) * half]
        logits = (
            jnp.einsum("qhd,khd->hqk", query_rows, key_tile, preferred_element_type=jnp.float32)
            * scaling
        )
        visible = key_pos[None, :] <= query_pos[part_idx * half : (part_idx + 1) * half][:, None]
        return (logits, visible[None])

    def fold_tile(running, key_tile, value_tile, key_pos):
        maxima, totals, weighted = running
        results = []
        for part_idx in range(2):
            lower = part_idx * half
            state = (
                maxima[:, lower : lower + half],
                totals[:, lower : lower + half],
                weighted[:, lower : lower + half],
            )

            def fold_active(current):
                old_max, old_tot, old_weighted = current
                logits, visible = tile_logits(part_idx, key_tile, key_pos)
                new_max = jnp.maximum(
                    old_max, jnp.max(jnp.where(visible, logits, -jnp.inf), axis=2)
                )
                expo = jnp.where(visible, jnp.exp(logits - new_max[..., None]), jnp.float32(0.0))
                rescale = jnp.exp(old_max - new_max)
                new_tot = old_tot * rescale + jnp.sum(expo, axis=2)
                new_weighted = old_weighted * rescale[..., None] + jnp.einsum(
                    "hqk,khd->hqd",
                    expo.astype(jnp.bfloat16),
                    value_tile,
                    preferred_element_type=jnp.float32,
                )
                return (new_max, new_tot, new_weighted)

            state = lax.cond(
                jnp.min(key_pos) <= query_last[part_idx],
                fold_active,
                lambda current: current,
                state,
            )
            results.append(state)
        return tuple(
            (jnp.concatenate([results[0][slot], results[1][slot]], axis=1) for slot in range(3))
        )

    def column_tile(key_tile, key_pos, maxima, totals):
        tile_len = key_tile.shape[0]
        sums = []
        for part_idx in range(2):
            lower = part_idx * half

            def column_active(unused):
                logits, visible = tile_logits(part_idx, key_tile, key_pos)
                expo = jnp.where(
                    visible,
                    jnp.exp(logits - maxima[:, lower : lower + half][..., None]),
                    jnp.float32(0.0),
                )
                return jnp.sum(expo / totals[:, lower : lower + half][..., None], axis=1)

            def masked(unused):
                return jnp.zeros((head_count, tile_len), jnp.float32)

            sums.append(
                lax.cond(jnp.min(key_pos) <= query_last[part_idx], column_active, masked, 0)
            )
        return sums[0] + sums[1]

    def column_rows(key_rows, begin_row, maxima, totals):
        length = key_rows.shape[0]
        tile_len = min(length, half)
        tiles = length // tile_len
        key_split = key_rows.reshape(tiles, tile_len, head_count, HEAD_DIM)

        def single(items):
            tile_idx, key_tile = items
            key_pos = layout_pos(
                begin_row + tile_idx * tile_len + jnp.arange(tile_len, dtype=jnp.int32)
            )
            return column_tile(key_tile, key_pos, maxima, totals)

        stacked_terms = lax.map(single, (jnp.arange(tiles, dtype=jnp.int32), key_split))
        return stacked_terms.transpose(1, 0, 2).reshape(head_count, length)

    initial = (
        jnp.full((head_count, row_count), -1e30, jnp.float32),
        jnp.zeros((head_count, row_count), jnp.float32),
        jnp.zeros((head_count, row_count, HEAD_DIM), jnp.float32),
    )
    running = initial
    key_piece = lax.all_gather(key_loc, "blk", axis=0, tiled=True)
    value_piece = lax.all_gather(value_loc, "blk", axis=0, tiled=True)
    length = key_piece.shape[0]
    tile_len = min(length, half)
    tiles = length // tile_len
    key_split = key_piece.reshape(tiles, tile_len, head_count, HEAD_DIM)
    value_split = value_piece.reshape(tiles, tile_len, head_count, HEAD_DIM)

    def inner(state, items):
        tile_idx, key_tile, value_tile = items
        key_pos = layout_pos(tile_idx * tile_len + jnp.arange(tile_len, dtype=jnp.int32))
        return (fold_tile(state, key_tile, value_tile, key_pos), None)

    running, unused = lax.scan(
        inner, running, (jnp.arange(tiles, dtype=jnp.int32), key_split, value_split)
    )
    maxima, totals, weighted = running

    def advance(step_idx, state):
        key_block, column_acc = state
        anchor = (my_block - step_idx) % block_total
        column_acc = column_acc + column_rows(key_block, anchor * row_count, maxima, totals)
        key_block = passed_along(key_block, "blk", 1)
        column_acc = passed_along(column_acc, "blk", 1)
        return (key_block, column_acc)

    unused_keys, heavy_scores = lax.fori_loop(
        0, block_total, advance, (key_loc, jnp.zeros((head_count, row_count), jnp.float32))
    )
    output = (
        (weighted / totals[..., None])
        .transpose(1, 0, 2)
        .reshape(row_count, head_count * HEAD_DIM)
        .astype(jnp.bfloat16)
    )
    later_rows = output[half:]
    for bit in range(bit_count):
        later_rows = partner(later_rows, "blk", bit)
    later_scores = heavy_scores[:, half:]
    for bit in range(bit_count):
        later_scores = partner(later_scores, "blk", bit)
    output = jnp.concatenate([output[:half], later_rows], axis=0)
    heavy_scores = jnp.concatenate([heavy_scores[:, :half], later_scores], axis=1)
    attended = lax.all_to_all(output, "head", split_axis=0, concat_axis=1, tiled=True)
    return (attended, heavy_scores)


def solution(mesh):
    placed = (P("blk", "head"), P("blk", "head"), P("blk", "head"))
    return jax.shard_map(
        local,
        mesh=mesh,
        in_specs=placed,
        out_specs=(P(("blk", "head"), None), P("head", "blk")),
        check_vma=False,
    )
```

profile of v0, /device:TPU:6, one launch (start us, length us, event | category | flops | bytes accessed | tf_op | source)
XLA Modules:
  0.0 1050.6 jit_solution(7527804805216113666)
XLA Ops:
  16.2 7.5 collective-permute-done.3
  23.7 5.1 collective-permute-start.4
  28.8 6.5 collective-permute-done.4
  35.3 15.7 %collective-permute-start.5 = (bf16[3,384,1,128]{3,1,2,0:T(8,128)(2,1)S(1)}, bf16[3,384,1,128]{3,1,2,0:T(8,128)(2,1)S(1)}, u32[]{:S(2)}, u32[]{:S(2)}) collective-permute-start(bf16[3,384,1,128]{3,1,2,0:T(8,128)(2,1)S(1)} %collective-permute-done.4), channel_id=1, source_target_pairs={{0,8},{1,9},{2,10},{3,11},{4,12},{5,13},{6,14},{7,15},{8,0},{9,1},... | collective-permute-start | bytes 884744 | tf_op jit(solution)/shard_map/ppermute | solution.py:14
  51.0 10.1 collective-permute-done.5
  63.4 119.9 %all-gather.3.cloned.1.call-done = bf16[12288,1,128]{2,0,1:T(8,128)(2,1)} async-done(((bf16[768,1,128]{2,0,1:T(8,128)(2,1)}), bf16[12288,1,128]{2,0,1:T(8,128)(2,1)}) %all-gather.3.cloned.1.call-update) | async-done | bytes 3145744 | tf_op jit(solution)/shard_map/all_gather | solution.py:142
  183.2 101.3 %all-gather.5.cloned.1.call-done = bf16[12288,1,128]{2,0,1:T(8,128)(2,1)} async-done(((bf16[768,1,128]{2,0,1:T(8,128)(2,1)}), bf16[12288,1,128]{2,0,1:T(8,128)(2,1)}) %all-gather.5.cloned.1.call-update) | async-done | bytes 3145744 | tf_op jit(solution)/shard_map/all_gather | solution.py:143
  284.6 205.1 %while.70 = (s32[]{:T(128)}, f32[1,768]{1,0:T(1,128)S(1)}, f32[1,768]{1,0:T(1,128)S(1)}, f32[1,768,128]{2,1,0:T(8,128)S(1)}, s32[32]{0:T(128)S(1)}, /*index=5*/s...) while((s32[]{:T(128)}, f32[1,768]{1,0:T(1,128)S(1)}, ...), condition=%wide.region_12.13_spmd.clone, body=%wide.region_2.12_spmd.clone.sunk | while | flops 154853760 | bytes 6987713 | solution.py:155
  499.9 3.9 collective-permute-start.8
  503.8 4.1 collective-permute-done.8
  509.8 14.7 %collective-permute-done.9 = bf16[384,128]{1,0:T(8,128)(2,1)S(1)} collective-permute-done((bf16[384,128]{1,0:T(8,128)(2,1)S(1)}, bf16[384,128]{1,0:T(8,128)(2,1)S(1)}, u32[]{:S(2)}, u32[]{:S(2)}) %collective-permute-start.9) | collective-permute-done | bytes 98336 | tf_op jit(solution)/shard_map/ppermute | solution.py:14
  525.2 5.0 all-to-all-start
  530.3 482.6 %while.72 = (s32[]{:T(128)}, bf16[768,1,128]{2,0,1:T(8,128)(2,1)S(1)}, f32[1,768]{1,0:T(1,128)S(1)}, s32[]{:T(128)}, s32[]{:T(128)}, /*index=5*/bf16[384,1,128]{...) while((s32[]{:T(128)}, ...), condition=%wide.region_23.24_spmd.clone, body=%wide.region_13.23_spmd.clone.sunk | while | flops 77288464 | bytes 1840971 | solution.py:168
  532.9 12.0 %while.73 = (s32[]{:T(128)}, f32[2,1,384]{2,1,0:T(1,128)S(1)}, s32[2]{0:T(128)S(1)}, s32[]{:T(128)}, s32[]{:T(128)}, /*index=5*/bf16[2,384,1,128]{3,1,2,0:T(8,12...) while((s32[]{:T(128)}, f32[2,1,384]{2,1,0:T(1,128)S(1)}, ...), condition=%wide.region_22.22_spmd, body=%wide.region_14.21_spmd.sunk | while | flops 77273856 | bytes 636237 | solution.py:133
  548.2 12.9 %collective-permute-done.1 = f32[1,768]{1,0:T(1,128)S(1)} collective-permute-done((f32[1,768]{1,0:T(1,128)S(1)}, f32[1,768]{1,0:T(1,128)S(1)}, u32[]{:S(2)}, u32[]{:S(2)}) %collective-permute-start.1) | collective-permute-done | bytes 3104 | tf_op jit(solution)/shard_map/while/body/eval_jaxpr/ppermute | solution.py:20
  563.8 11.6 %while.73 = (s32[]{:T(128)}, f32[2,1,384]{2,1,0:T(1,128)S(1)}, s32[2]{0:T(128)S(1)}, s32[]{:T(128)}, s32[]{:T(128)}, /*index=5*/bf16[2,384,1,128]{3,1,2,0:T(8,12...) while((s32[]{:T(128)}, f32[2,1,384]{2,1,0:T(1,128)S(1)}, ...), condition=%wide.region_22.22_spmd, body=%wide.region_14.21_spmd.sunk | while | flops 77273856 | bytes 636237 | solution.py:133
  577.4 14.2 %collective-permute-done.1 = f32[1,768]{1,0:T(1,128)S(1)} collective-permute-done((f32[1,768]{1,0:T(1,128)S(1)}, f32[1,768]{1,0:T(1,128)S(1)}, u32[]{:S(2)}, u32[]{:S(2)}) %collective-permute-start.1) | collective-permute-done | bytes 3104 | tf_op jit(solution)/shard_map/while/body/eval_jaxpr/ppermute | solution.py:20
  594.2 11.6 %while.73 = (s32[]{:T(128)}, f32[2,1,384]{2,1,0:T(1,128)S(1)}, s32[2]{0:T(128)S(1)}, s32[]{:T(128)}, s32[]{:T(128)}, /*index=5*/bf16[2,384,1,128]{3,1,2,0:T(8,12...) while((s32[]{:T(128)}, f32[2,1,384]{2,1,0:T(1,128)S(1)}, ...), condition=%wide.region_22.22_spmd, body=%wide.region_14.21_spmd.sunk | while | flops 77273856 | bytes 636237 | solution.py:133
  607.8 14.2 %collective-permute-done.1 = f32[1,768]{1,0:T(1,128)S(1)} collective-permute-done((f32[1,768]{1,0:T(1,128)S(1)}, f32[1,768]{1,0:T(1,128)S(1)}, u32[]{:S(2)}, u32[]{:S(2)}) %collective-permute-start.1) | collective-permute-done | bytes 3104 | tf_op jit(solution)/shard_map/while/body/eval_jaxpr/ppermute | solution.py:20
  624.7 11.6 %while.73 = (s32[]{:T(128)}, f32[2,1,384]{2,1,0:T(1,128)S(1)}, s32[2]{0:T(128)S(1)}, s32[]{:T(128)}, s32[]{:T(128)}, /*index=5*/bf16[2,384,1,128]{3,1,2,0:T(8,12...) while((s32[]{:T(128)}, f32[2,1,384]{2,1,0:T(1,128)S(1)}, ...), condition=%wide.region_22.22_spmd, body=%wide.region_14.21_spmd.sunk | while | flops 77273856 | bytes 636237 | solution.py:133
  638.3 13.8 %collective-permute-done.1 = f32[1,768]{1,0:T(1,128)S(1)} collective-permute-done((f32[1,768]{1,0:T(1,128)S(1)}, f32[1,768]{1,0:T(1,128)S(1)}, u32[]{:S(2)}, u32[]{:S(2)}) %collective-permute-start.1) | collective-permute-done | bytes 3104 | tf_op jit(solution)/shard_map/while/body/eval_jaxpr/ppermute | solution.py:20
  654.7 11.6 %while.73 = (s32[]{:T(128)}, f32[2,1,384]{2,1,0:T(1,128)S(1)}, s32[2]{0:T(128)S(1)}, s32[]{:T(128)}, s32[]{:T(128)}, /*index=5*/bf16[2,384,1,128]{3,1,2,0:T(8,12...) while((s32[]{:T(128)}, f32[2,1,384]{2,1,0:T(1,128)S(1)}, ...), condition=%wide.region_22.22_spmd, body=%wide.region_14.21_spmd.sunk | while | flops 77273856 | bytes 636237 | solution.py:133
  668.3 13.8 %collective-permute-done.1 = f32[1,768]{1,0:T(1,128)S(1)} collective-permute-done((f32[1,768]{1,0:T(1,128)S(1)}, f32[1,768]{1,0:T(1,128)S(1)}, u32[]{:S(2)}, u32[]{:S(2)}) %collective-permute-start.1) | collective-permute-done | bytes 3104 | tf_op jit(solution)/shard_map/while/body/eval_jaxpr/ppermute | solution.py:20
  684.8 11.6 %while.73 = (s32[]{:T(128)}, f32[2,1,384]{2,1,0:T(1,128)S(1)}, s32[2]{0:T(128)S(1)}, s32[]{:T(128)}, s32[]{:T(128)}, /*index=5*/bf16[2,384,1,128]{3,1,2,0:T(8,12...) while((s32[]{:T(128)}, f32[2,1,384]{2,1,0:T(1,128)S(1)}, ...), condition=%wide.region_22.22_spmd, body=%wide.region_14.21_spmd.sunk | while | flops 77273856 | bytes 636237 | solution.py:133
  698.4 13.8 %collective-permute-done.1 = f32[1,768]{1,0:T(1,128)S(1)} collective-permute-done((f32[1,768]{1,0:T(1,128)S(1)}, f32[1,768]{1,0:T(1,128)S(1)}, u32[]{:S(2)}, u32[]{:S(2)}) %collective-permute-start.1) | collective-permute-done | bytes 3104 | tf_op jit(solution)/shard_map/while/body/eval_jaxpr/ppermute | solution.py:20
  714.9 11.6 %while.73 = (s32[]{:T(128)}, f32[2,1,384]{2,1,0:T(1,128)S(1)}, s32[2]{0:T(128)S(1)}, s32[]{:T(128)}, s32[]{:T(128)}, /*index=5*/bf16[2,384,1,128]{3,1,2,0:T(8,12...) while((s32[]{:T(128)}, f32[2,1,384]{2,1,0:T(1,128)S(1)}, ...), condition=%wide.region_22.22_spmd, body=%wide.region_14.21_spmd.sunk | while | flops 77273856 | bytes 636237 | solution.py:133
  728.5 13.8 %collective-permute-done.1 = f32[1,768]{1,0:T(1,128)S(1)} collective-permute-done((f32[1,768]{1,0:T(1,128)S(1)}, f32[1,768]{1,0:T(1,128)S(1)}, u32[]{:S(2)}, u32[]{:S(2)}) %collective-permute-start.1) | collective-permute-done | bytes 3104 | tf_op jit(solution)/shard_map/while/body/eval_jaxpr/ppermute | solution.py:20
  744.9 11.6 %while.73 = (s32[]{:T(128)}, f32[2,1,384]{2,1,0:T(1,128)S(1)}, s32[2]{0:T(128)S(1)}, s32[]{:T(128)}, s32[]{:T(128)}, /*index=5*/bf16[2,384,1,128]{3,1,2,0:T(8,12...) while((s32[]{:T(128)}, f32[2,1,384]{2,1,0:T(1,128)S(1)}, ...), condition=%wide.region_22.22_spmd, body=%wide.region_14.21_spmd.sunk | while | flops 77273856 | bytes 636237 | solution.py:133
  758.5 13.8 %collective-permute-done.1 = f32[1,768]{1,0:T(1,128)S(1)} collective-permute-done((f32[1,768]{1,0:T(1,128)S(1)}, f32[1,768]{1,0:T(1,128)S(1)}, u32[]{:S(2)}, u32[]{:S(2)}) %collective-permute-start.1) | collective-permute-done | bytes 3104 | tf_op jit(solution)/shard_map/while/body/eval_jaxpr/ppermute | solution.py:20
  775.0 11.6 %while.73 = (s32[]{:T(128)}, f32[2,1,384]{2,1,0:T(1,128)S(1)}, s32[2]{0:T(128)S(1)}, s32[]{:T(128)}, s32[]{:T(128)}, /*index=5*/bf16[2,384,1,128]{3,1,2,0:T(8,12...) while((s32[]{:T(128)}, f32[2,1,384]{2,1,0:T(1,128)S(1)}, ...), condition=%wide.region_22.22_spmd, body=%wide.region_14.21_spmd.sunk | while | flops 77273856 | bytes 636237 | solution.py:133
  788.6 13.8 %collective-permute-done.1 = f32[1,768]{1,0:T(1,128)S(1)} collective-permute-done((f32[1,768]{1,0:T(1,128)S(1)}, f32[1,768]{1,0:T(1,128)S(1)}, u32[]{:S(2)}, u32[]{:S(2)}) %collective-permute-start.1) | collective-permute-done | bytes 3104 | tf_op jit(solution)/shard_map/while/body/eval_jaxpr/ppermute | solution.py:20
  805.1 11.6 %while.73 = (s32[]{:T(128)}, f32[2,1,384]{2,1,0:T(1,128)S(1)}, s32[2]{0:T(128)S(1)}, s32[]{:T(128)}, s32[]{:T(128)}, /*index=5*/bf16[2,384,1,128]{3,1,2,0:T(8,12...) while((s32[]{:T(128)}, f32[2,1,384]{2,1,0:T(1,128)S(1)}, ...), condition=%wide.region_22.22_spmd, body=%wide.region_14.21_spmd.sunk | while | flops 77273856 | bytes 636237 | solution.py:133
  818.7 13.8 %collective-permute-done.1 = f32[1,768]{1,0:T(1,128)S(1)} collective-permute-done((f32[1,768]{1,0:T(1,128)S(1)}, f32[1,768]{1,0:T(1,128)S(1)}, u32[]{:S(2)}, u32[]{:S(2)}) %collective-permute-start.1) | collective-permute-done | bytes 3104 | tf_op jit(solution)/shard_map/while/body/eval_jaxpr/ppermute | solution.py:20
  835.1 11.6 %while.73 = (s32[]{:T(128)}, f32[2,1,384]{2,1,0:T(1,128)S(1)}, s32[2]{0:T(128)S(1)}, s32[]{:T(128)}, s32[]{:T(128)}, /*index=5*/bf16[2,384,1,128]{3,1,2,0:T(8,12...) while((s32[]{:T(128)}, f32[2,1,384]{2,1,0:T(1,128)S(1)}, ...), condition=%wide.region_22.22_spmd, body=%wide.region_14.21_spmd.sunk | while | flops 77273856 | bytes 636237 | solution.py:133
  848.7 13.8 %collective-permute-done.1 = f32[1,768]{1,0:T(1,128)S(1)} collective-permute-done((f32[1,768]{1,0:T(1,128)S(1)}, f32[1,768]{1,0:T(1,128)S(1)}, u32[]{:S(2)}, u32[]{:S(2)}) %collective-permute-start.1) | collective-permute-done | bytes 3104 | tf_op jit(solution)/shard_map/while/body/eval_jaxpr/ppermute | solution.py:20
  865.2 11.6 %while.73 = (s32[]{:T(128)}, f32[2,1,384]{2,1,0:T(1,128)S(1)}, s32[2]{0:T(128)S(1)}, s32[]{:T(128)}, s32[]{:T(128)}, /*index=5*/bf16[2,384,1,128]{3,1,2,0:T(8,12...) while((s32[]{:T(128)}, f32[2,1,384]{2,1,0:T(1,128)S(1)}, ...), condition=%wide.region_22.22_spmd, body=%wide.region_14.21_spmd.sunk | while | flops 77273856 | bytes 636237 | solution.py:133
  878.8 13.8 %collective-permute-done.1 = f32[1,768]{1,0:T(1,128)S(1)} collective-permute-done((f32[1,768]{1,0:T(1,128)S(1)}, f32[1,768]{1,0:T(1,128)S(1)}, u32[]{:S(2)}, u32[]{:S(2)}) %collective-permute-start.1) | collective-permute-done | bytes 3104 | tf_op jit(solution)/shard_map/while/body/eval_jaxpr/ppermute | solution.py:20
  895.3 11.6 %while.73 = (s32[]{:T(128)}, f32[2,1,384]{2,1,0:T(1,128)S(1)}, s32[2]{0:T(128)S(1)}, s32[]{:T(128)}, s32[]{:T(128)}, /*index=5*/bf16[2,384,1,128]{3,1,2,0:T(8,12...) while((s32[]{:T(128)}, f32[2,1,384]{2,1,0:T(1,128)S(1)}, ...), condition=%wide.region_22.22_spmd, body=%wide.region_14.21_spmd.sunk | while | flops 77273856 | bytes 636237 | solution.py:133
  908.9 13.8 %collective-permute-done.1 = f32[1,768]{1,0:T(1,128)S(1)} collective-permute-done((f32[1,768]{1,0:T(1,128)S(1)}, f32[1,768]{1,0:T(1,128)S(1)}, u32[]{:S(2)}, u32[]{:S(2)}) %collective-permute-start.1) | collective-permute-done | bytes 3104 | tf_op jit(solution)/shard_map/while/body/eval_jaxpr/ppermute | solution.py:20
  925.3 11.6 %while.73 = (s32[]{:T(128)}, f32[2,1,384]{2,1,0:T(1,128)S(1)}, s32[2]{0:T(128)S(1)}, s32[]{:T(128)}, s32[]{:T(128)}, /*index=5*/bf16[2,384,1,128]{3,1,2,0:T(8,12...) while((s32[]{:T(128)}, f32[2,1,384]{2,1,0:T(1,128)S(1)}, ...), condition=%wide.region_22.22_spmd, body=%wide.region_14.21_spmd.sunk | while | flops 77273856 | bytes 636237 | solution.py:133
  938.9 13.8 %collective-permute-done.1 = f32[1,768]{1,0:T(1,128)S(1)} collective-permute-done((f32[1,768]{1,0:T(1,128)S(1)}, f32[1,768]{1,0:T(1,128)S(1)}, u32[]{:S(2)}, u32[]{:S(2)}) %collective-permute-start.1) | collective-permute-done | bytes 3104 | tf_op jit(solution)/shard_map/while/body/eval_jaxpr/ppermute | solution.py:20
  955.4 11.6 %while.73 = (s32[]{:T(128)}, f32[2,1,384]{2,1,0:T(1,128)S(1)}, s32[2]{0:T(128)S(1)}, s32[]{:T(128)}, s32[]{:T(128)}, /*index=5*/bf16[2,384,1,128]{3,1,2,0:T(8,12...) while((s32[]{:T(128)}, f32[2,1,384]{2,1,0:T(1,128)S(1)}, ...), condition=%wide.region_22.22_spmd, body=%wide.region_14.21_spmd.sunk | while | flops 77273856 | bytes 636237 | solution.py:133
  969.0 13.8 %collective-permute-done.1 = f32[1,768]{1,0:T(1,128)S(1)} collective-permute-done((f32[1,768]{1,0:T(1,128)S(1)}, f32[1,768]{1,0:T(1,128)S(1)}, u32[]{:S(2)}, u32[]{:S(2)}) %collective-permute-start.1) | collective-permute-done | bytes 3104 | tf_op jit(solution)/shard_map/while/body/eval_jaxpr/ppermute | solution.py:20
  985.5 11.6 %while.73 = (s32[]{:T(128)}, f32[2,1,384]{2,1,0:T(1,128)S(1)}, s32[2]{0:T(128)S(1)}, s32[]{:T(128)}, s32[]{:T(128)}, /*index=5*/bf16[2,384,1,128]{3,1,2,0:T(8,12...) while((s32[]{:T(128)}, f32[2,1,384]{2,1,0:T(1,128)S(1)}, ...), condition=%wide.region_22.22_spmd, body=%wide.region_14.21_spmd.sunk | while | flops 77273856 | bytes 636237 | solution.py:133
  999.1 13.8 %collective-permute-done.1 = f32[1,768]{1,0:T(1,128)S(1)} collective-permute-done((f32[1,768]{1,0:T(1,128)S(1)}, f32[1,768]{1,0:T(1,128)S(1)}, u32[]{:S(2)}, u32[]{:S(2)}) %collective-permute-start.1) | collective-permute-done | bytes 3104 | tf_op jit(solution)/shard_map/while/body/eval_jaxpr/ppermute | solution.py:20
  1023.3 5.0 collective-permute-done.12
  1028.3 7.4 collective-permute-start.13
  1035.7 6.8 collective-permute-done.13
  (1106 shorter events, 340.6 us)
Async XLA Ops:
  7.2 176.1 %all-gather.3.cloned.1.call-start = ((), (), s32[]{:S(2)}) async-start(), calls=%async_computation.1 | async-start | bytes 3342336 | tf_op jit(solution)/shard_map/all_gather | solution.py:142
  9.3 3.5 collective-permute-start.2
  12.8 10.9 %collective-permute-start.3 = (bf16[3,384,1,128]{3,1,2,0:T(8,128)(2,1)S(1)}, bf16[3,384,1,128]{3,1,2,0:T(8,128)(2,1)S(1)}, u32[]{:S(2)}, u32[]{:S(2)}) collective-permute-start(bf16[3,384,1,128]{3,1,2,0:T(8,128)(2,1)S(1)} %collective-permute-done.2), channel_id=1, source_target_pairs={{0,2},{1,3},{2,0},{3,1},{4,6},{5,7},{6,4},{7,5},{8,10},{9,11},{10,... | collective-permute-start | bytes 884744 | tf_op jit(solution)/shard_map/ppermute | solution.py:14
  23.7 11.6 %collective-permute-start.4 = (bf16[3,384,1,128]{3,1,2,0:T(8,128)(2,1)S(1)}, bf16[3,384,1,128]{3,1,2,0:T(8,128)(2,1)S(1)}, u32[]{:S(2)}, u32[]{:S(2)}) collective-permute-start(bf16[3,384,1,128]{3,1,2,0:T(8,128)(2,1)S(1)} %collective-permute-done.3), channel_id=1, source_target_pairs={{0,4},{1,5},{2,6},{3,7},{4,0},{5,1},{6,2},{7,3},{8,12},{9,13},{10,... | collective-permute-start | bytes 884744 | tf_op jit(solution)/shard_map/ppermute | solution.py:14
  35.3 25.8 %collective-permute-start.5 = (bf16[3,384,1,128]{3,1,2,0:T(8,128)(2,1)S(1)}, bf16[3,384,1,128]{3,1,2,0:T(8,128)(2,1)S(1)}, u32[]{:S(2)}, u32[]{:S(2)}) collective-permute-start(bf16[3,384,1,128]{3,1,2,0:T(8,128)(2,1)S(1)} %collective-permute-done.4), channel_id=1, source_target_pairs={{0,8},{1,9},{2,10},{3,11},{4,12},{5,13},{6,14},{7,15},{8,0},{9,1},... | collective-permute-start | bytes 884744 | tf_op jit(solution)/shard_map/ppermute | solution.py:14
  61.8 222.7 %all-gather.5.cloned.1.call-start = ((), (), s32[]{:S(2)}) async-start(), calls=%async_computation.2 | async-start | bytes 3342336 | tf_op jit(solution)/shard_map/all_gather | solution.py:143
  284.6 245.7 %copy-start = (bf16[768,1,128]{2,0,1:T(8,128)(2,1)S(1)}, bf16[768,1,128]{2,0,1:T(8,128)(2,1)}, u32[]{:S(2)}) copy-start(bf16[768,1,128]{2,0,1:T(8,128)(2,1)} %pad_maximum_fusion.4) | copy-start | bytes 589828
  489.9 3.2 collective-permute-start.6
  493.1 6.8 collective-permute-start.7
  499.9 8.0 collective-permute-start.8
  507.9 16.6 %collective-permute-start.9 = (bf16[384,128]{1,0:T(8,128)(2,1)S(1)}, bf16[384,128]{1,0:T(8,128)(2,1)S(1)}, u32[]{:S(2)}, u32[]{:S(2)}) collective-permute-start(bf16[384,128]{1,0:T(8,128)(2,1)S(1)} %collective-permute-done.8), channel_id=1, source_target_pairs={{0,8},{1,9},{2,10},{3,11},{4,12},{5,13},{6,14},{7,15},{8,0},{9,1},... | collective-permute-start | bytes 294920 | tf_op jit(solution)/shard_map/ppermute | solution.py:14
  525.2 517.9 %all-to-all-start = ((bf16[32,24,128]{2,1,0:T(8,128)(2,1)}), bf16[32,24,128]{2,1,0:T(8,128)(2,1)S(1)}, u32[]{:S(2)}, u32[]{:S(2)}) async-start(bf16[32,24,128]{2,1,0:T(8,128)(2,1)} %bitcast.30), calls=%async_computation | async-start | bytes 393216 | tf_op jit(solution)/shard_map/all_to_all | solution.py:185
  531.0 30.2 %collective-permute-start = (bf16[768,1,128]{2,0,1:T(8,128)(2,1)}, bf16[768,1,128]{2,0,1:T(8,128)(2,1)S(1)}, u32[]{:S(2)}, u32[]{:S(2)}) collective-permute-start(bf16[768,1,128]{2,0,1:T(8,128)(2,1)} %copy.57), channel_id=1, source_target_pairs={{0,1},{1,2},{2,3},{3,4},{4,5},{5,6},{6,7},{7,8},{8,9},{9,10},{10,1... | collective-permute-start | bytes 589832 | tf_op jit(solution)/shard_map/while/body/eval_jaxpr/ppermute | solution.py:20
  545.0 16.1 %collective-permute-start.1 = (f32[1,768]{1,0:T(1,128)S(1)}, f32[1,768]{1,0:T(1,128)S(1)}, u32[]{:S(2)}, u32[]{:S(2)}) collective-permute-start(f32[1,768]{1,0:T(1,128)S(1)} %add.496), channel_id=1, source_target_pairs={{0,1},{1,2},{2,3},{3,4},{4,5},{5,6},{6,7},{7,8},{8,9},{9,10},{10,1... | collective-permute-start | bytes 9224 | tf_op jit(solution)/shard_map/while/body/eval_jaxpr/ppermute | solution.py:20
  561.8 29.8 %collective-permute-start = (bf16[768,1,128]{2,0,1:T(8,128)(2,1)}, bf16[768,1,128]{2,0,1:T(8,128)(2,1)S(1)}, u32[]{:S(2)}, u32[]{:S(2)}) collective-permute-start(bf16[768,1,128]{2,0,1:T(8,128)(2,1)} %copy.57), channel_id=1, source_target_pairs={{0,1},{1,2},{2,3},{3,4},{4,5},{5,6},{6,7},{7,8},{8,9},{9,10},{10,1... | collective-permute-start | bytes 589832 | tf_op jit(solution)/shard_map/while/body/eval_jaxpr/ppermute | solution.py:20
  575.4 16.1 %collective-permute-start.1 = (f32[1,768]{1,0:T(1,128)S(1)}, f32[1,768]{1,0:T(1,128)S(1)}, u32[]{:S(2)}, u32[]{:S(2)}) collective-permute-start(f32[1,768]{1,0:T(1,128)S(1)} %add.496), channel_id=1, source_target_pairs={{0,1},{1,2},{2,3},{3,4},{4,5},{5,6},{6,7},{7,8},{8,9},{9,10},{10,1... | collective-permute-start | bytes 9224 | tf_op jit(solution)/shard_map/while/body/eval_jaxpr/ppermute | solution.py:20
  592.2 29.8 %collective-permute-start = (bf16[768,1,128]{2,0,1:T(8,128)(2,1)}, bf16[768,1,128]{2,0,1:T(8,128)(2,1)S(1)}, u32[]{:S(2)}, u32[]{:S(2)}) collective-permute-start(bf16[768,1,128]{2,0,1:T(8,128)(2,1)} %copy.57), channel_id=1, source_target_pairs={{0,1},{1,2},{2,3},{3,4},{4,5},{5,6},{6,7},{7,8},{8,9},{9,10},{10,1... | collective-permute-start | bytes 589832 | tf_op jit(solution)/shard_map/while/body/eval_jaxpr/ppermute | solution.py:20
  605.9 16.1 %collective-permute-start.1 = (f32[1,768]{1,0:T(1,128)S(1)}, f32[1,768]{1,0:T(1,128)S(1)}, u32[]{:S(2)}, u32[]{:S(2)}) collective-permute-start(f32[1,768]{1,0:T(1,128)S(1)} %add.496), channel_id=1, source_target_pairs={{0,1},{1,2},{2,3},{3,4},{4,5},{5,6},{6,7},{7,8},{8,9},{9,10},{10,1... | collective-permute-start | bytes 9224 | tf_op jit(solution)/shard_map/while/body/eval_jaxpr/ppermute | solution.py:20
  622.7 29.4 %collective-permute-start = (bf16[768,1,128]{2,0,1:T(8,128)(2,1)}, bf16[768,1,128]{2,0,1:T(8,128)(2,1)S(1)}, u32[]{:S(2)}, u32[]{:S(2)}) collective-permute-start(bf16[768,1,128]{2,0,1:T(8,128)(2,1)} %copy.57), channel_id=1, source_target_pairs={{0,1},{1,2},{2,3},{3,4},{4,5},{5,6},{6,7},{7,8},{8,9},{9,10},{10,1... | collective-permute-start | bytes 589832 | tf_op jit(solution)/shard_map/while/body/eval_jaxpr/ppermute | solution.py:20
  636.3 15.7 %collective-permute-start.1 = (f32[1,768]{1,0:T(1,128)S(1)}, f32[1,768]{1,0:T(1,128)S(1)}, u32[]{:S(2)}, u32[]{:S(2)}) collective-permute-start(f32[1,768]{1,0:T(1,128)S(1)} %add.496), channel_id=1, source_target_pairs={{0,1},{1,2},{2,3},{3,4},{4,5},{5,6},{6,7},{7,8},{8,9},{9,10},{10,1... | collective-permute-start | bytes 9224 | tf_op jit(solution)/shard_map/while/body/eval_jaxpr/ppermute | solution.py:20
  652.8 29.4 %collective-permute-start = (bf16[768,1,128]{2,0,1:T(8,128)(2,1)}, bf16[768,1,128]{2,0,1:T(8,128)(2,1)S(1)}, u32[]{:S(2)}, u32[]{:S(2)}) collective-permute-start(bf16[768,1,128]{2,0,1:T(8,128)(2,1)} %copy.57), channel_id=1, source_target_pairs={{0,1},{1,2},{2,3},{3,4},{4,5},{5,6},{6,7},{7,8},{8,9},{9,10},{10,1... | collective-permute-start | bytes 589832 | tf_op jit(solution)/shard_map/while/body/eval_jaxpr/ppermute | solution.py:20
  666.4 15.7 %collective-permute-start.1 = (f32[1,768]{1,0:T(1,128)S(1)}, f32[1,768]{1,0:T(1,128)S(1)}, u32[]{:S(2)}, u32[]{:S(2)}) collective-permute-start(f32[1,768]{1,0:T(1,128)S(1)} %add.496), channel_id=1, source_target_pairs={{0,1},{1,2},{2,3},{3,4},{4,5},{5,6},{6,7},{7,8},{8,9},{9,10},{10,1... | collective-permute-start | bytes 9224 | tf_op jit(solution)/shard_map/while/body/eval_jaxpr/ppermute | solution.py:20
  682.8 29.4 %collective-permute-start = (bf16[768,1,128]{2,0,1:T(8,128)(2,1)}, bf16[768,1,128]{2,0,1:T(8,128)(2,1)S(1)}, u32[]{:S(2)}, u32[]{:S(2)}) collective-permute-start(bf16[768,1,128]{2,0,1:T(8,128)(2,1)} %copy.57), channel_id=1, source_target_pairs={{0,1},{1,2},{2,3},{3,4},{4,5},{5,6},{6,7},{7,8},{8,9},{9,10},{10,1... | collective-permute-start | bytes 589832 | tf_op jit(solution)/shard_map/while/body/eval_jaxpr/ppermute | solution.py:20
  696.5 15.7 %collective-permute-start.1 = (f32[1,768]{1,0:T(1,128)S(1)}, f32[1,768]{1,0:T(1,128)S(1)}, u32[]{:S(2)}, u32[]{:S(2)}) collective-permute-start(f32[1,768]{1,0:T(1,128)S(1)} %add.496), channel_id=1, source_target_pairs={{0,1},{1,2},{2,3},{3,4},{4,5},{5,6},{6,7},{7,8},{8,9},{9,10},{10,1... | collective-permute-start | bytes 9224 | tf_op jit(solution)/shard_map/while/body/eval_jaxpr/ppermute | solution.py:20
  712.9 29.4 %collective-permute-start = (bf16[768,1,128]{2,0,1:T(8,128)(2,1)}, bf16[768,1,128]{2,0,1:T(8,128)(2,1)S(1)}, u32[]{:S(2)}, u32[]{:S(2)}) collective-permute-start(bf16[768,1,128]{2,0,1:T(8,128)(2,1)} %copy.57), channel_id=1, source_target_pairs={{0,1},{1,2},{2,3},{3,4},{4,5},{5,6},{6,7},{7,8},{8,9},{9,10},{10,1... | collective-permute-start | bytes 589832 | tf_op jit(solution)/shard_map/while/body/eval_jaxpr/ppermute | solution.py:20
  726.5 15.7 %collective-permute-start.1 = (f32[1,768]{1,0:T(1,128)S(1)}, f32[1,768]{1,0:T(1,128)S(1)}, u32[]{:S(2)}, u32[]{:S(2)}) collective-permute-start(f32[1,768]{1,0:T(1,128)S(1)} %add.496), channel_id=1, source_target_pairs={{0,1},{1,2},{2,3},{3,4},{4,5},{5,6},{6,7},{7,8},{8,9},{9,10},{10,1... | collective-permute-start | bytes 9224 | tf_op jit(solution)/shard_map/while/body/eval_jaxpr/ppermute | solution.py:20
  743.0 29.4 %collective-permute-start = (bf16[768,1,128]{2,0,1:T(8,128)(2,1)}, bf16[768,1,128]{2,0,1:T(8,128)(2,1)S(1)}, u32[]{:S(2)}, u32[]{:S(2)}) collective-permute-start(bf16[768,1,128]{2,0,1:T(8,128)(2,1)} %copy.57), channel_id=1, source_target_pairs={{0,1},{1,2},{2,3},{3,4},{4,5},{5,6},{6,7},{7,8},{8,9},{9,10},{10,1... | collective-permute-start | bytes 589832 | tf_op jit(solution)/shard_map/while/body/eval_jaxpr/ppermute | solution.py:20
  756.6 15.7 %collective-permute-start.1 = (f32[1,768]{1,0:T(1,128)S(1)}, f32[1,768]{1,0:T(1,128)S(1)}, u32[]{:S(2)}, u32[]{:S(2)}) collective-permute-start(f32[1,768]{1,0:T(1,128)S(1)} %add.496), channel_id=1, source_target_pairs={{0,1},{1,2},{2,3},{3,4},{4,5},{5,6},{6,7},{7,8},{8,9},{9,10},{10,1... | collective-permute-start | bytes 9224 | tf_op jit(solution)/shard_map/while/body/eval_jaxpr/ppermute | solution.py:20
  773.0 29.4 %collective-permute-start = (bf16[768,1,128]{2,0,1:T(8,128)(2,1)}, bf16[768,1,128]{2,0,1:T(8,128)(2,1)S(1)}, u32[]{:S(2)}, u32[]{:S(2)}) collective-permute-start(bf16[768,1,128]{2,0,1:T(8,128)(2,1)} %copy.57), channel_id=1, source_target_pairs={{0,1},{1,2},{2,3},{3,4},{4,5},{5,6},{6,7},{7,8},{8,9},{9,10},{10,1... | collective-permute-start | bytes 589832 | tf_op jit(solution)/shard_map/while/body/eval_jaxpr/ppermute | solution.py:20
  786.7 15.7 %collective-permute-start.1 = (f32[1,768]{1,0:T(1,128)S(1)}, f32[1,768]{1,0:T(1,128)S(1)}, u32[]{:S(2)}, u32[]{:S(2)}) collective-permute-start(f32[1,768]{1,0:T(1,128)S(1)} %add.496), channel_id=1, source_target_pairs={{0,1},{1,2},{2,3},{3,4},{4,5},{5,6},{6,7},{7,8},{8,9},{9,10},{10,1... | collective-permute-start | bytes 9224 | tf_op jit(solution)/shard_map/while/body/eval_jaxpr/ppermute | solution.py:20
  803.1 29.4 %collective-permute-start = (bf16[768,1,128]{2,0,1:T(8,128)(2,1)}, bf16[768,1,128]{2,0,1:T(8,128)(2,1)S(1)}, u32[]{:S(2)}, u32[]{:S(2)}) collective-permute-start(bf16[768,1,128]{2,0,1:T(8,128)(2,1)} %copy.57), channel_id=1, source_target_pairs={{0,1},{1,2},{2,3},{3,4},{4,5},{5,6},{6,7},{7,8},{8,9},{9,10},{10,1... | collective-permute-start | bytes 589832 | tf_op jit(solution)/shard_map/while/body/eval_jaxpr/ppermute | solution.py:20
  816.7 15.7 %collective-permute-start.1 = (f32[1,768]{1,0:T(1,128)S(1)}, f32[1,768]{1,0:T(1,128)S(1)}, u32[]{:S(2)}, u32[]{:S(2)}) collective-permute-start(f32[1,768]{1,0:T(1,128)S(1)} %add.496), channel_id=1, source_target_pairs={{0,1},{1,2},{2,3},{3,4},{4,5},{5,6},{6,7},{7,8},{8,9},{9,10},{10,1... | collective-permute-start | bytes 9224 | tf_op jit(solution)/shard_map/while/body/eval_jaxpr/ppermute | solution.py:20
  833.2 29.4 %collective-permute-start = (bf16[768,1,128]{2,0,1:T(8,128)(2,1)}, bf16[768,1,128]{2,0,1:T(8,128)(2,1)S(1)}, u32[]{:S(2)}, u32[]{:S(2)}) collective-permute-start(bf16[768,1,128]{2,0,1:T(8,128)(2,1)} %copy.57), channel_id=1, source_target_pairs={{0,1},{1,2},{2,3},{3,4},{4,5},{5,6},{6,7},{7,8},{8,9},{9,10},{10,1... | collective-permute-start | bytes 589832 | tf_op jit(solution)/shard_map/while/body/eval_jaxpr/ppermute | solution.py:20
  846.8 15.7 %collective-permute-start.1 = (f32[1,768]{1,0:T(1,128)S(1)}, f32[1,768]{1,0:T(1,128)S(1)}, u32[]{:S(2)}, u32[]{:S(2)}) collective-permute-start(f32[1,768]{1,0:T(1,128)S(1)} %add.496), channel_id=1, source_target_pairs={{0,1},{1,2},{2,3},{3,4},{4,5},{5,6},{6,7},{7,8},{8,9},{9,10},{10,1... | collective-permute-start | bytes 9224 | tf_op jit(solution)/shard_map/while/body/eval_jaxpr/ppermute | solution.py:20
  863.2 29.4 %collective-permute-start = (bf16[768,1,128]{2,0,1:T(8,128)(2,1)}, bf16[768,1,128]{2,0,1:T(8,128)(2,1)S(1)}, u32[]{:S(2)}, u32[]{:S(2)}) collective-permute-start(bf16[768,1,128]{2,0,1:T(8,128)(2,1)} %copy.57), channel_id=1, source_target_pairs={{0,1},{1,2},{2,3},{3,4},{4,5},{5,6},{6,7},{7,8},{8,9},{9,10},{10,1... | collective-permute-start | bytes 589832 | tf_op jit(solution)/shard_map/while/body/eval_jaxpr/ppermute | solution.py:20
  876.9 15.7 %collective-permute-start.1 = (f32[1,768]{1,0:T(1,128)S(1)}, f32[1,768]{1,0:T(1,128)S(1)}, u32[]{:S(2)}, u32[]{:S(2)}) collective-permute-start(f32[1,768]{1,0:T(1,128)S(1)} %add.496), channel_id=1, source_target_pairs={{0,1},{1,2},{2,3},{3,4},{4,5},{5,6},{6,7},{7,8},{8,9},{9,10},{10,1... | collective-permute-start | bytes 9224 | tf_op jit(solution)/shard_map/while/body/eval_jaxpr/ppermute | solution.py:20
  893.3 29.4 %collective-permute-start = (bf16[768,1,128]{2,0,1:T(8,128)(2,1)}, bf16[768,1,128]{2,0,1:T(8,128)(2,1)S(1)}, u32[]{:S(2)}, u32[]{:S(2)}) collective-permute-start(bf16[768,1,128]{2,0,1:T(8,128)(2,1)} %copy.57), channel_id=1, source_target_pairs={{0,1},{1,2},{2,3},{3,4},{4,5},{5,6},{6,7},{7,8},{8,9},{9,10},{10,1... | collective-permute-start | bytes 589832 | tf_op jit(solution)/shard_map/while/body/eval_jaxpr/ppermute | solution.py:20
  906.9 15.7 %collective-permute-start.1 = (f32[1,768]{1,0:T(1,128)S(1)}, f32[1,768]{1,0:T(1,128)S(1)}, u32[]{:S(2)}, u32[]{:S(2)}) collective-permute-start(f32[1,768]{1,0:T(1,128)S(1)} %add.496), channel_id=1, source_target_pairs={{0,1},{1,2},{2,3},{3,4},{4,5},{5,6},{6,7},{7,8},{8,9},{9,10},{10,1... | collective-permute-start | bytes 9224 | tf_op jit(solution)/shard_map/while/body/eval_jaxpr/ppermute | solution.py:20
  923.4 29.4 %collective-permute-start = (bf16[768,1,128]{2,0,1:T(8,128)(2,1)}, bf16[768,1,128]{2,0,1:T(8,128)(2,1)S(1)}, u32[]{:S(2)}, u32[]{:S(2)}) collective-permute-start(bf16[768,1,128]{2,0,1:T(8,128)(2,1)} %copy.57), channel_id=1, source_target_pairs={{0,1},{1,2},{2,3},{3,4},{4,5},{5,6},{6,7},{7,8},{8,9},{9,10},{10,1... | collective-permute-start | bytes 589832 | tf_op jit(solution)/shard_map/while/body/eval_jaxpr/ppermute | solution.py:20
  937.0 15.7 %collective-permute-start.1 = (f32[1,768]{1,0:T(1,128)S(1)}, f32[1,768]{1,0:T(1,128)S(1)}, u32[]{:S(2)}, u32[]{:S(2)}) collective-permute-start(f32[1,768]{1,0:T(1,128)S(1)} %add.496), channel_id=1, source_target_pairs={{0,1},{1,2},{2,3},{3,4},{4,5},{5,6},{6,7},{7,8},{8,9},{9,10},{10,1... | collective-permute-start | bytes 9224 | tf_op jit(solution)/shard_map/while/body/eval_jaxpr/ppermute | solution.py:20
  953.4 29.4 %collective-permute-start = (bf16[768,1,128]{2,0,1:T(8,128)(2,1)}, bf16[768,1,128]{2,0,1:T(8,128)(2,1)S(1)}, u32[]{:S(2)}, u32[]{:S(2)}) collective-permute-start(bf16[768,1,128]{2,0,1:T(8,128)(2,1)} %copy.57), channel_id=1, source_target_pairs={{0,1},{1,2},{2,3},{3,4},{4,5},{5,6},{6,7},{7,8},{8,9},{9,10},{10,1... | collective-permute-start | bytes 589832 | tf_op jit(solution)/shard_map/while/body/eval_jaxpr/ppermute | solution.py:20
  967.1 15.7 %collective-permute-start.1 = (f32[1,768]{1,0:T(1,128)S(1)}, f32[1,768]{1,0:T(1,128)S(1)}, u32[]{:S(2)}, u32[]{:S(2)}) collective-permute-start(f32[1,768]{1,0:T(1,128)S(1)} %add.496), channel_id=1, source_target_pairs={{0,1},{1,2},{2,3},{3,4},{4,5},{5,6},{6,7},{7,8},{8,9},{9,10},{10,1... | collective-permute-start | bytes 9224 | tf_op jit(solution)/shard_map/while/body/eval_jaxpr/ppermute | solution.py:20
  983.5 29.4 %collective-permute-start = (bf16[768,1,128]{2,0,1:T(8,128)(2,1)}, bf16[768,1,128]{2,0,1:T(8,128)(2,1)S(1)}, u32[]{:S(2)}, u32[]{:S(2)}) collective-permute-start(bf16[768,1,128]{2,0,1:T(8,128)(2,1)} %copy.57), channel_id=1, source_target_pairs={{0,1},{1,2},{2,3},{3,4},{4,5},{5,6},{6,7},{7,8},{8,9},{9,10},{10,1... | collective-permute-start | bytes 589832 | tf_op jit(solution)/shard_map/while/body/eval_jaxpr/ppermute | solution.py:20
  997.1 15.7 %collective-permute-start.1 = (f32[1,768]{1,0:T(1,128)S(1)}, f32[1,768]{1,0:T(1,128)S(1)}, u32[]{:S(2)}, u32[]{:S(2)}) collective-permute-start(f32[1,768]{1,0:T(1,128)S(1)} %add.496), channel_id=1, source_target_pairs={{0,1},{1,2},{2,3},{3,4},{4,5},{5,6},{6,7},{7,8},{8,9},{9,10},{10,1... | collective-permute-start | bytes 9224 | tf_op jit(solution)/shard_map/while/body/eval_jaxpr/ppermute | solution.py:20
  1012.9 3.0 collective-permute-start.10
  1015.9 5.5 collective-permute-start.11
  1021.4 7.0 collective-permute-start.12
  1028.3 14.2 %collective-permute-start.13 = (f32[1,384]{1,0:T(1,128)S(1)}, f32[1,384]{1,0:T(1,128)S(1)}, u32[]{:S(2)}, u32[]{:S(2)}) collective-permute-start(f32[1,384]{1,0:T(1,128)S(1)} %collective-permute-done.12), channel_id=1, source_target_pairs={{0,8},{1,9},{2,10},{3,11},{4,12},{5,13},{6,14},{7,15},{8,0},{9,1},... | collective-permute-start | bytes 4616 | tf_op jit(solution)/shard_map/ppermute | solution.py:14
Sparse Core Ops, SparseCore 0:
  62.0 121.2 all-gather.2
  186.5 97.9 all-gather.4
where the time goes:
time: 1060 us; the launch traced here: 1050 us
  waiting for transfers between devices  508 us (48%)
  loops' own time  207 us (20%)
  starting transfers between devices  118 us (11%)
  local copies, waits for them, and re-layouts  115 us (11%)
  other arithmetic  55.5 us (5%)
  matrix products  33.9 us (3%)
  between operations  14.2 us (1%)
    ppermute x32, waiting for transfers between devices, passed_along(): return lax.ppermute(value, axis, pairs)  221 us
    all_gather x1, waiting for transfers between devices, local(): key_piece = lax.all_gather(key_loc, 'blk', axis=0, tiled=True)  120 us
    another operation x16, loops' own time, column_rows(): lax.map(single, (jnp.arange(tiles, dtype=jnp.int32), key_split))  103 us
    all_gather x1, waiting for transfers between devices, local(): value_piece = lax.all_gather(value_loc, 'blk', axis=0, tiled=True)  101 us
    another operation x1, loops' own time, local(): lax.scan(inner, running, (jnp.arange(tiles, dtype=jnp.int32), key_split,...  100 us
    ppermute x12, waiting for transfers between devices, partner(): return lax.ppermute(value, axis, pairs)  65.8 us
    ppermute x32, starting transfers between devices, passed_along(): return lax.ppermute(value, axis, pairs)  62.5 us
    ppermute x12, starting transfers between devices, partner(): return lax.ppermute(value, axis, pairs)  50.3 us
  transfers between devices with their start and end apart: 47, of which 30 were waited for; matrix products, arithmetic and copies ran while one was open for 9% of the time, Pallas kernels for 0%

commit v1 on v0

v1 whole, which is shorter than its diff:
```python
import functools
import math

import jax
import jax.numpy as jnp
from jax import lax
from jax.experimental import pallas as pl
from jax.experimental.pallas import tpu as pltpu
from jax.sharding import PartitionSpec as P

MESH = pl.DeviceIdType.MESH
DIM = 128
ROWS = 768
HEADS = 32
HALF = 8
CHUNK = 192
CHUNKS = ROWS // CHUNK
GROUP = ROWS // HEADS
GROUPS = CHUNK // GROUP
TILE = 384
WIDE = 1536
SCALE = math.log2(math.e) / math.sqrt(DIM)
LOW = -1e30


def dot_rows(a, b):
    return lax.dot_general(a, b, (((1,), (1,)), ((), ())), preferred_element_type=jnp.float32)


def dot(a, b):
    return lax.dot_general(a, b, (((1,), (0,)), ((), ())), preferred_element_type=jnp.float32)


def fold_lanes(value, op):
    out = value[:, :128]
    for u in range(1, value.shape[1] // 128):
        out = op(out, value[:, u * 128 : (u + 1) * 128])
    return out


def weigh(logits, values):
    top = jnp.max(fold_lanes(logits, jnp.maximum), axis=1, keepdims=True)
    expo = jnp.exp2((logits - top) * SCALE)
    total = fold_lanes(expo, jnp.add)
    weights = expo.astype(jnp.bfloat16)
    return top, total, weights, dot(weights, values)


def to_lanes(column):
    out = []
    for begin, size in ((0, 128), (128, 64)):
        part = column[begin : begin + size]
        row = lax.broadcasted_iota(jnp.int32, part.shape, 0)
        lane = lax.broadcasted_iota(jnp.int32, part.shape, 1)
        out.append(jnp.sum(jnp.where(row == lane, part, 0.0), axis=0, keepdims=True))
    return out


def to_column(row):
    parts = []
    for begin, size in ((0, 128), (128, 64)):
        square = jnp.broadcast_to(row[:, begin : begin + 128], (128, 128))
        parts.append(jnp.transpose(square)[:size])
    return jnp.concatenate(parts, axis=0)


def kernel(
    q_ref, k_ref, v_ref, att_ref, heavy_ref,
    keys, values, q_far, weights_tri, top_tri, total_tri, out_tri,
    weights_far, top_far, total_far, out_far, lse_col,
    send_own, send_far, stat_own, stat_far, stat_peer,
    got_own, got_far, got_stat_own, got_stat_far, turned_a, turned_b,
    column, column_out, column_in,
    k_send, k_recv, v_send, v_recv, q_send, q_recv,
    own_send, own_recv, own_stat_send, own_stat_recv,
    far_send, far_recv, far_stat_send, far_stat_recv,
    peer_send, peer_recv, col_send, col_recv,
):
    h = lax.axis_index("head")
    b = lax.axis_index("blk")
    later = b // HALF
    w = lax.rem(b, HALF)
    y, core = w // 2, lax.rem(w, 2)
    x, z = h // 8, lax.rem(h, 8)
    base = later * HALF
    is_early, is_late = later == 0, later == 1

    def place(dy, flip):
        yy = lax.rem(y + dy, 4)
        return yy * 2 + (lax.rem(core + flip, 2))

    def half_device(block):
        return (h, base + block)

    partner = (h, w + (1 - later) * HALF)
    w_right, w_left, w_core = place(1, 0), place(3, 0), place(0, 1)

    def copy(src, dst, send_sem, recv_sem, device):
        return pltpu.make_async_remote_copy(
            src_ref=src, dst_ref=dst, send_sem=send_sem, recv_sem=recv_sem,
            device_id=device, device_id_type=MESH,
        )

    barrier = pltpu.get_barrier_semaphore()

    def greet(device):
        pl.semaphore_signal(barrier, inc=1, device_id=device, device_id_type=MESH)

    def greet_far(j, carry):
        greet((lax.rem(h + j, HEADS), w + (1 - later) * HALF))
        return carry

    def greet_heads(j, carry):
        greet((lax.rem(h + j, HEADS), b))
        return carry

    def greet_half(j, carry):
        greet((h, base + lax.rem(w + j, HALF)))
        return carry

    lax.fori_loop(0, HEADS, greet_far, 0)
    lax.fori_loop(1, HEADS, greet_heads, 0)
    lax.fori_loop(1, HALF, greet_half, 0)

    keys[w] = k_ref[...]
    values[w] = v_ref[...]

    def triangle(block, masked):
        for t in range(ROWS // TILE):
            rows = pl.ds(t * TILE, TILE)
            logits = dot_rows(q_ref[rows, :], keys[block])
            if masked:
                row = lax.broadcasted_iota(jnp.int32, logits.shape, 0) + t * TILE
                col = lax.broadcasted_iota(jnp.int32, logits.shape, 1)
                logits = jnp.where(col <= row, logits, LOW)
            top, total, weights, out = weigh(logits, values[block])
            weights_tri[block, rows, :] = weights
            top_tri[block, rows, :] = jnp.broadcast_to(top, (TILE, 128))
            total_tri[block, rows, :] = total
            out_tri[block, rows, :] = out

    triangle(w, True)
    column[...] = jnp.zeros_like(column)

    pl.semaphore_wait(barrier, 2 * HEADS - 1 + HALF - 1)

    def q_copy(ci):
        rows = pl.ds(pl.multiple_of(ci * CHUNK, CHUNK), CHUNK)
        return copy(q_ref.at[rows], q_far.at[rows], q_send.at[ci], q_recv.at[ci], partner)

    @pl.when(is_late)
    def _():
        def start(i, carry):
            q_copy(lax.rem(x + i, CHUNKS)).start()
            return carry

        lax.fori_loop(0, CHUNKS, start, 0)

    def k_copy(block, slot, to):
        return copy(keys.at[block], keys.at[block], k_send.at[slot], k_recv.at[block], half_device(to))

    def v_copy(block, slot, to):
        return copy(values.at[block], values.at[block], v_send.at[slot], v_recv.at[block], half_device(to))

    k_copy(w, 0, w_right).start()
    k_copy(w, 1, w_left).start()
    k_copy(w, 2, w_core).start()
    v_copy(w, 0, w_right).start()
    v_copy(w, 1, w_left).start()
    v_copy(w, 2, w_core).start()

    def k_wait(block):
        k_copy(block, 0, w_core).wait_recv()

    def v_wait(block):
        v_copy(block, 0, w_core).wait_recv()

    def own_copy(hg):
        return copy(send_own.at[hg], got_own.at[h], own_send.at[hg], own_recv.at[h], (hg, b))

    def own_stat_copy(hg):
        return copy(
            stat_own.at[hg // GROUPS], got_stat_own.at[h],
            own_stat_send.at[hg], own_stat_recv.at[h], (hg, b),
        )

    def far_copy(hg):
        return copy(send_far.at[hg], got_far.at[h], far_send.at[hg], far_recv.at[h], (hg, w + HALF))

    def far_stat_copy(hg):
        return copy(
            stat_far.at[hg // GROUPS], got_stat_far.at[h],
            far_stat_send.at[hg], far_stat_recv.at[h], (hg, w + HALF),
        )

    def peer_copy(stat, ci):
        return copy(stat.at[ci], stat_peer.at[ci], peer_send.at[ci], peer_recv.at[ci], partner)

    def settle(count, rows, tops, totals, outs):
        top = lax.fori_loop(
            1, count, lambda j, top: jnp.maximum(top, tops[j, rows, :]), tops[0, rows, :]
        )

        def add(j, carry):
            total, out = carry
            factor = jnp.exp2((tops[j, rows, :] - top) * SCALE)
            return (total + factor * totals[j, rows, :], out + factor * outs[j, rows, :])

        zero = jnp.zeros((CHUNK, 128), jnp.float32)
        total, out = lax.fori_loop(0, count, add, (zero, zero))
        total = jnp.sum(total, axis=1, keepdims=True)
        return out * (1.0 / total), top * SCALE + jnp.log2(total)

    def settle_triangle():
        def chunk(ci, carry):
            rows = pl.ds(pl.multiple_of(ci * CHUNK, CHUNK), CHUNK)
            out, lse = settle(w + 1, rows, top_tri, total_tri, out_tri)
            send_own[pl.ds(ci * GROUPS, GROUPS)] = out.reshape(GROUPS, GROUP, DIM).astype(jnp.bfloat16)
            lse_col[rows, :] = lse
            low, high = to_lanes(lse)
            stat_own[ci, :, :128] = low
            stat_own[ci, :, 128:] = high
            return carry

        lax.fori_loop(0, CHUNKS, chunk, 0)

        @pl.when(is_late)
        def _():
            for ci in range(CHUNKS):
                peer_copy(stat_own, ci).start()

        got_own[h] = send_own[h]

        def start(j, carry):
            hg = lax.rem(h + j, HEADS)
            own_copy(hg).start()

            @pl.when(is_late)
            def _():
                own_stat_copy(hg).start()

            return carry

        lax.fori_loop(1, HEADS, start, 0)

        @pl.when(is_late)
        def _():
            got_stat_own[h] = stat_own[h // GROUPS]

    def rectangle(ci):
        q_copy(ci).wait_recv()
        rows = pl.ds(pl.multiple_of(ci * CHUNK, CHUNK), CHUNK)
        local = pl.ds(0, CHUNK)

        def step(d, carry):
            key_tile = keys[pl.ds(d * 2, 2)].reshape(WIDE, DIM)
            value_tile = values[pl.ds(d * 2, 2)].reshape(WIDE, DIM)
            logits = dot_rows(q_far[rows, :], key_tile)
            top, total, weights, out = weigh(logits, value_tile)
            weights_far[d, rows, :] = weights
            top_far[d, rows, :] = jnp.broadcast_to(top, (CHUNK, 128))
            total_far[d, local, :] = total
            out_far[d, local, :] = out
            return carry

        lax.fori_loop(0, HALF // 2, step, 0)
        top = top_far[0, rows, :]
        for d in range(1, HALF // 2):
            top = jnp.maximum(top, top_far[d, rows, :])
        total = jnp.zeros((CHUNK, 128), jnp.float32)
        out = jnp.zeros((CHUNK, 128), jnp.float32)
        for d in range(HALF // 2):
            factor = jnp.exp2((top_far[d, rows, :] - top) * SCALE)
            total = total + factor * total_far[d]
            out = out + factor * out_far[d]
        total = jnp.sum(total, axis=1, keepdims=True)
        out = out * (1.0 / total)
        send_far[pl.ds(ci * GROUPS, GROUPS)] = out.reshape(GROUPS, GROUP, DIM).astype(jnp.bfloat16)
        low, high = to_lanes(top * SCALE + jnp.log2(total))
        stat_far[ci, :, :128] = low
        stat_far[ci, :, 128:] = high

        def start(g, carry):
            hg = ci * GROUPS + lax.rem(z + g, GROUPS)
            far_copy(hg).start()
            far_stat_copy(hg).start()
            return carry

        lax.fori_loop(0, GROUPS, start, 0)
        peer_copy(stat_far, ci).start()

    def step(i, carry):
        @pl.when(i == 1)
        def _():
            k_wait(w_core)
            v_wait(w_core)

        @pl.when(i == 2)
        def _():
            k_wait(w_left)
            k_copy(w_left, 3, w_right).start()
            k_copy(w_left, 4, w_core).start()
            k_wait(w_right)
            k_copy(w_right, 5, w_core).start()
            v_wait(w_right)
            v_copy(w_right, 3, w_left).start()
            v_copy(w_right, 5, w_core).start()
            v_wait(w_left)
            v_copy(w_left, 4, w_core).start()

        @pl.when(i == 4)
        def _():
            for dy in (3, 1):
                k_wait(place(dy, 1))
                v_wait(place(dy, 1))

        @pl.when(i == 5)
        def _():
            far_block = place(2, 0)
            k_wait(far_block)
            k_copy(far_block, 6, w_core).start()
            v_wait(far_block)
            v_copy(far_block, 6, w_core).start()
            k_wait(place(2, 1))
            v_wait(place(2, 1))

        @pl.when(jnp.logical_and(is_early, i >= 5))
        def _():
            rectangle(lax.rem(x + i - 5, CHUNKS))

        dy = jnp.where(i == 1, 0, jnp.where(i >= 6, 2, jnp.where(lax.rem(i, 2) == 0, 3, 1)))
        flip = jnp.where(jnp.logical_or(i == 1, jnp.logical_or(i == 4, jnp.logical_or(i == 5, i == 7))), 1, 0)
        block = place(dy, flip)

        @pl.when(jnp.logical_and(i < 8, block < w))
        def _():
            triangle(block, False)

        @pl.when(i == 7)
        def _():
            settle_triangle()

        return carry

    lax.fori_loop(1, 9, step, 0)

    def add_columns(count, rows, tops, weights, lse, width):
        per = width // ROWS

        def tile(j, carry):
            factor = jnp.exp2(tops[j, rows, :] * SCALE - lse)
            for u in range(width // 128):
                part = weights[j, rows, u * 128 : (u + 1) * 128].astype(jnp.float32) * factor
                part = jnp.sum(part.reshape(CHUNK // 8, 8, 128), axis=0)
                lanes = slice(u % 6 * 128, u % 6 * 128 + 128)
                column[j * per + u // 6, :, lanes] += part
            return carry

        lax.fori_loop(0, count, tile, 0)

    def both(one, two):
        top = jnp.maximum(one, two)
        return top + jnp.log2(jnp.exp2(one - top) + jnp.exp2(two - top))

    def columns(i, carry):
        ci = lax.rem(x + i, CHUNKS)
        rows = pl.ds(pl.multiple_of(ci * CHUNK, CHUNK), CHUNK)
        peer_copy(stat_own, ci).wait_recv()

        @pl.when(is_early)
        def _():
            add_columns(w + 1, rows, top_tri, weights_tri, lse_col[rows, :], ROWS)
            lse = to_column(both(stat_far[ci], stat_peer[ci]))
            add_columns(HALF // 2, rows, top_far, weights_far, lse, WIDE)

        @pl.when(is_late)
        def _():
            lse = to_column(both(stat_own[ci], stat_peer[ci]))
            add_columns(w + 1, rows, top_tri, weights_tri, lse, ROWS)

        return carry

    lax.fori_loop(0, CHUNKS, columns, 0)
    for j in range(HALF):
        column_out[j] = jnp.sum(column[j], axis=0, keepdims=True)

    def col_copy(block):
        return copy(
            column_out.at[block], column_in.at[w], col_send.at[block], col_recv.at[w], half_device(block)
        )

    def col_start(j, carry):
        col_copy(lax.rem(w + j, HALF)).start()
        return carry

    lax.fori_loop(1, HALF, col_start, 0)
    column_in[w] = column_out[w]

    def arrived(j, carry):
        hg = lax.rem(h + j, HEADS)
        copy(send_own.at[hg], got_own.at[hg], own_send.at[hg], own_recv.at[hg], (hg, b)).wait_recv()
        return carry

    lax.fori_loop(1, HEADS, arrived, 0)

    @pl.when(is_early)
    def _():
        for hh in range(HEADS):
            att_ref[:, hh * 128 : (hh + 1) * 128] = got_own[hh]

    @pl.when(is_late)
    def _():
        def stat_arrived(j, carry):
            hg = lax.rem(h + j, HEADS)
            copy(
                stat_own.at[0], got_stat_own.at[hg], own_stat_send.at[hg], own_stat_recv.at[hg], (hg, b)
            ).wait_recv()
            return carry

        lax.fori_loop(1, HEADS, stat_arrived, 0)

        def far_arrived(j, carry):
            hg = lax.rem(h + j, HEADS)
            device = (hg, w)
            copy(send_far.at[hg], got_far.at[hg], far_send.at[hg], far_recv.at[hg], device).wait_recv()
            copy(
                stat_far.at[0], got_stat_far.at[hg], far_stat_send.at[hg], far_stat_recv.at[hg], device
            ).wait_recv()
            return carry

        lax.fori_loop(0, HEADS, far_arrived, 0)
        pad = jnp.zeros((128 - HEADS, 256), jnp.float32)
        stat_a = jnp.concatenate([got_stat_own[hh] for hh in range(HEADS)] + [pad], axis=0)
        stat_b = jnp.concatenate([got_stat_far[hh] for hh in range(HEADS)] + [pad], axis=0)
        turned_a[...] = jnp.transpose(stat_a)
        turned_b[...] = jnp.transpose(stat_b)
        mine = pl.ds(pl.multiple_of(z * GROUP, 8), GROUP)
        lse_a, lse_b = turned_a[mine, :], turned_b[mine, :]
        share_a = 1.0 / (1.0 + jnp.exp2(lse_b - lse_a))
        share_b = 1.0 / (1.0 + jnp.exp2(lse_a - lse_b))
        for hh in range(HEADS):
            merged = (
                got_own[hh].astype(jnp.float32) * share_a[:, hh : hh + 1]
                + got_far[hh].astype(jnp.float32) * share_b[:, hh : hh + 1]
            )
            att_ref[:, hh * 128 : (hh + 1) * 128] = merged.astype(jnp.bfloat16)

    def col_arrived(j, carry):
        block = lax.rem(w + j, HALF)
        copy(
            column_out.at[block], column_in.at[block], col_send.at[block], col_recv.at[block],
            half_device(block),
        ).wait_recv()
        return carry

    lax.fori_loop(1, HALF, col_arrived, 0)
    heavy = column_in[0]
    for j in range(1, HALF):
        heavy = heavy + column_in[j]
    heavy_ref[...] = heavy

    for slot in range(7):
        k_copy(w, slot, w_core).wait_send()
        v_copy(w, slot, w_core).wait_send()

    def own_left(j, carry):
        hg = lax.rem(h + j, HEADS)
        own_copy(hg).wait_send()

        @pl.when(is_late)
        def _():
            own_stat_copy(hg).wait_send()

        return carry

    lax.fori_loop(1, HEADS, own_left, 0)

    @pl.when(is_early)
    def _():
        def far_left(hg, carry):
            far_copy(hg).wait_send()
            far_stat_copy(hg).wait_send()
            return carry

        lax.fori_loop(0, HEADS, far_left, 0)

    def chunk_left(ci, carry):
        peer_copy(stat_own, ci).wait_send()

        @pl.when(is_late)
        def _():
            q_copy(ci).wait_send()

        return carry

    lax.fori_loop(0, CHUNKS, chunk_left, 0)

    def col_left(j, carry):
        col_copy(lax.rem(w + j, HALF)).wait_send()
        return carry

    lax.fori_loop(1, HALF, col_left, 0)


def local(queries, key_states, value_states):
    bf16, f32 = jnp.bfloat16, jnp.float32
    vmem, dma = pltpu.VMEM, pltpu.SemaphoreType.DMA
    whole = pl.BlockSpec(memory_space=pltpu.VMEM)
    quarter = HALF // 2
    return pl.pallas_call(
        kernel,
        out_shape=(
            jax.ShapeDtypeStruct((GROUP, HEADS * DIM), bf16),
            jax.ShapeDtypeStruct((1, ROWS), f32),
        ),
        in_specs=[whole] * 3,
        out_specs=(whole, whole),
        scratch_shapes=[
            vmem((HALF, ROWS, DIM), bf16),
            vmem((HALF, ROWS, DIM), bf16),
            vmem((ROWS, DIM), bf16),
            vmem((HALF, ROWS, ROWS), bf16),
            vmem((HALF, ROWS, 128), f32),
            vmem((HALF, ROWS, 128), f32),
            vmem((HALF, ROWS, DIM), f32),
            vmem((quarter, ROWS, WIDE), bf16),
            vmem((quarter, ROWS, 128), f32),
            vmem((quarter, CHUNK, 128), f32),
            vmem((quarter, CHUNK, DIM), f32),
            vmem((ROWS, 128), f32),
            vmem((HEADS, GROUP, DIM), bf16),
            vmem((HEADS, GROUP, DIM), bf16),
            vmem((CHUNKS, 1, 256), f32),
            vmem((CHUNKS, 1, 256), f32),
            vmem((CHUNKS, 1, 256), f32),
            vmem((HEADS, GROUP, DIM), bf16),
            vmem((HEADS, GROUP, DIM), bf16),
            vmem((HEADS, 1, 256), f32),
            vmem((HEADS, 1, 256), f32),
            vmem((256, 128), f32),
            vmem((256, 128), f32),
            vmem((HALF, 8, ROWS), f32),
            vmem((HALF, 1, ROWS), f32),
            vmem((HALF, 1, ROWS), f32),
            dma((7,)), dma((HALF,)), dma((7,)), dma((HALF,)), dma((CHUNKS,)), dma((CHUNKS,)),
            dma((HEADS,)), dma((HEADS,)), dma((HEADS,)), dma((HEADS,)),
            dma((HEADS,)), dma((HEADS,)), dma((HEADS,)), dma((HEADS,)),
            dma((CHUNKS,)), dma((CHUNKS,)), dma((HALF,)), dma((HALF,)),
        ],
        compiler_params=pltpu.CompilerParams(
            collective_id=0, has_side_effects=True, vmem_limit_bytes=58 * 1024 * 1024
        ),
    )(queries, key_states, value_states)


def solution(mesh):
    placed = (P("blk", "head"), P("blk", "head"), P("blk", "head"))
    return jax.shard_map(
        local,
        mesh=mesh,
        in_specs=placed,
        out_specs=(P(("blk", "head"), None), P("head", "blk")),
        check_vma=False,
    )
```

time: 1060 us -> 72.1 us (0.07)
  the two profiles are of different devices: /device:TPU:6 before, /device:TPU:1 now
where the time goes in v1:
time: 72.1 us; the launch traced here: 71.9 us
  Pallas kernels  69.1 us (96%)
  local copies, waits for them, and re-layouts  2.2 us (3%)
    pallas_call x1, Pallas kernels, local(): pl.pallas_call(kernel, out_shape=(jax.ShapeDtypeStruct((GROUP, HEADS * DI...  69.1 us
    unnamed x4, local copies, waits for them, and re-layouts  2.2 us

profile of v1, /device:TPU:1, one launch (start us, length us, event | category | flops | bytes accessed | tf_op | source)
XLA Modules:
  0.0 71.9 jit_solution(1131646323132104671)
XLA Ops:
  0.6 69.1 %shard_map.50 = (bf16[24,4096]{1,0:T(8,128)(2,1)}, f32[1,768]{1,0:T(1,128)}) custom-call(bf16[768,128]{1,0:T(8,128)(2,1)} %q_ref.1, bf16[768,128]{1,0:T(8,128)(2,1)} %k_ref.1, bf16[768,128]{1,0:T(8,128)(2,1)} %v_ref.1), custom_call_target="tpu_custom_call" | custom-call | tf_op jit(solution)/shard_map/pallas_call | solution.py:510
  69.7 0.0 copy-start
  69.7 1.6 %copy.7 = bf16[24,4096]{1,0:T(8,128)(2,1)} copy(bf16[24,4096]{1,0:T(8,128)(2,1)} %get-tuple-element.4) | data formatting | bytes 393216
  71.3 0.0 copy-done
  71.3 0.6 copy.8
Async XLA Ops:
  69.7 1.6 %copy-start = (f32[1,768]{1,0:T(1,128)S(1)}, f32[1,768]{1,0:T(1,128)}, u32[]{:S(2)}) copy-start(f32[1,768]{1,0:T(1,128)} %get-tuple-element.5) | copy-start | bytes 9220

commit v2 on v1

--- a/solution.py
+++ b/solution.py
@@ -56,6 +56,13 @@
     return out
 
 
+def to_groups(column):
+    parts = column.reshape(GROUPS, GROUP, 128)
+    row = lax.broadcasted_iota(jnp.int32, parts.shape, 1)
+    lane = lax.broadcasted_iota(jnp.int32, parts.shape, 2)
+    return jnp.sum(jnp.where(row == lane, parts, 0.0), axis=1, keepdims=True)
+
+
 def to_column(row):
     parts = []
     for begin, size in ((0, 128), (128, 64)):
@@ -69,12 +76,12 @@
     keys, values, q_far, weights_tri, top_tri, total_tri, out_tri,
     weights_far, top_far, total_far, out_far, lse_col,
     send_own, send_far, stat_own, stat_far, stat_peer,
-    got_own, got_far, got_stat_own, got_stat_far, turned_a, turned_b,
+    tag_own, tag_far, got_own, got_far, got_stat_own, got_stat_far,
     column, column_out, column_in,
     k_send, k_recv, v_send, v_recv, q_send, q_recv,
     own_send, own_recv, own_stat_send, own_stat_recv,
     far_send, far_recv, far_stat_send, far_stat_recv,
-    peer_send, peer_recv, col_send, col_recv,
+    peer_send, peer_recv, col_send, col_recv, ready,
 ):
     h = lax.axis_index("head")
     b = lax.axis_index("blk")
@@ -106,27 +113,38 @@
     def greet(device):
         pl.semaphore_signal(barrier, inc=1, device_id=device, device_id_type=MESH)
 
-    def greet_far(j, carry):
-        greet((lax.rem(h + j, HEADS), w + (1 - later) * HALF))
-        return carry
-
-    def greet_heads(j, carry):
-        greet((lax.rem(h + j, HEADS), b))
-        return carry
-
-    def greet_half(j, carry):
-        greet((h, base + lax.rem(w + j, HALF)))
-        return carry
-
-    lax.fori_loop(0, HEADS, greet_far, 0)
-    lax.fori_loop(1, HEADS, greet_heads, 0)
-    lax.fori_loop(1, HALF, greet_half, 0)
+    def along_z(step):
+        return ((z >= step, (h - step, b)), (z + step < 8, (h + step, b)))
+
+    def along_x():
+        return [(lax.rem(h + 8 * d, HEADS), b) for d in (1, 2, 3)]
+
+    def count_z(step):
+        return (z >= step).astype(jnp.int32) + (z + step < 8).astype(jnp.int32)
+
+    for exists, device in along_z(1):
+        pl.when(exists)(functools.partial(greet, device))
+    for device in along_x():
+        greet(device)
+    for block in (w_right, w_left, w_core):
+        greet(half_device(block))
+    pl.when(is_early)(functools.partial(greet, partner))
+
+    def tell(index, device):
+        pl.semaphore_signal(ready.at[index], inc=1, device_id=device, device_id_type=MESH)
+
+    def tell_z(index, step):
+        for exists, device in along_z(step):
+            pl.when(exists)(functools.partial(tell, index, device))
+
+    def hear(index, count):
+        pl.semaphore_wait(ready.at[index], count)
 
     keys[w] = k_ref[...]
     values[w] = v_ref[...]
 
-    def triangle(block, masked):
-        for t in range(ROWS // TILE):
+    def triangle(block, masked, tiles):
+        for t in tiles:
             rows = pl.ds(t * TILE, TILE)
             logits = dot_rows(q_ref[rows, :], keys[block])
             if masked:
@@ -139,10 +157,7 @@
             total_tri[block, rows, :] = total
             out_tri[block, rows, :] = out
 
-    triangle(w, True)
-    column[...] = jnp.zeros_like(column)
-
-    pl.semaphore_wait(barrier, 2 * HEADS - 1 + HALF - 1)
+    pl.semaphore_wait(barrier, 6 + count_z(1) + later)
 
     def q_copy(ci):
         rows = pl.ds(pl.multiple_of(ci * CHUNK, CHUNK), CHUNK)
@@ -169,6 +184,15 @@
     v_copy(w, 1, w_left).start()
     v_copy(w, 2, w_core).start()
 
+    tell_z(0, 1)
+    triangle(w, True, (0,))
+    hear(0, count_z(1))
+    tell_z(1, 2)
+    triangle(w, True, (1,))
+    hear(1, count_z(2))
+    tell_z(2, 4)
+    column[...] = jnp.zeros_like(column)
+
     def k_wait(block):
         k_copy(block, 0, w_core).wait_recv()
 
@@ -176,21 +200,21 @@
         v_copy(block, 0, w_core).wait_recv()
 
     def own_copy(hg):
-        return copy(send_own.at[hg], got_own.at[h], own_send.at[hg], own_recv.at[h], (hg, b))
+        return copy(send_own.at[hg], got_own.at[h], own_send.at[0], own_recv.at[0], (hg, b))
 
     def own_stat_copy(hg):
         return copy(
-            stat_own.at[hg // GROUPS], got_stat_own.at[h],
-            own_stat_send.at[hg], own_stat_recv.at[h], (hg, b),
+            tag_own.at[hg], got_stat_own.at[h],
+            own_stat_send.at[0], own_stat_recv.at[0], (hg, b),
         )
 
     def far_copy(hg):
-        return copy(send_far.at[hg], got_far.at[h], far_send.at[hg], far_recv.at[h], (hg, w + HALF))
+        return copy(send_far.at[hg], got_far.at[h], far_send.at[0], far_recv.at[0], (hg, w + HALF))
 
     def far_stat_copy(hg):
         return copy(
-            stat_far.at[hg // GROUPS], got_stat_far.at[h],
-            far_stat_send.at[hg], far_stat_recv.at[h], (hg, w + HALF),
+            tag_far.at[hg], got_stat_far.at[h],
+            far_stat_send.at[0], far_stat_recv.at[0], (hg, w + HALF),
         )
 
     def peer_copy(stat, ci):
@@ -217,6 +241,7 @@
             out, lse = settle(w + 1, rows, top_tri, total_tri, out_tri)
             send_own[pl.ds(ci * GROUPS, GROUPS)] = out.reshape(GROUPS, GROUP, DIM).astype(jnp.bfloat16)
             lse_col[rows, :] = lse
+            tag_own[pl.ds(ci * GROUPS, GROUPS)] = to_groups(lse)
             low, high = to_lanes(lse)
             stat_own[ci, :, :128] = low
             stat_own[ci, :, 128:] = high
@@ -245,7 +270,7 @@
 
         @pl.when(is_late)
         def _():
-            got_stat_own[h] = stat_own[h // GROUPS]
+            got_stat_own[h] = tag_own[h]
 
     def rectangle(ci):
         q_copy(ci).wait_recv()
@@ -263,7 +288,7 @@
             out_far[d, local, :] = out
             return carry
 
-        lax.fori_loop(0, HALF // 2, step, 0)
+        lax.fori_loop(0, HALF // 2, step, 0, unroll=2)
         top = top_far[0, rows, :]
         for d in range(1, HALF // 2):
             top = jnp.maximum(top, top_far[d, rows, :])
@@ -276,7 +301,9 @@
         total = jnp.sum(total, axis=1, keepdims=True)
         out = out * (1.0 / total)
         send_far[pl.ds(ci * GROUPS, GROUPS)] = out.reshape(GROUPS, GROUP, DIM).astype(jnp.bfloat16)
-        low, high = to_lanes(top * SCALE + jnp.log2(total))
+        lse = top * SCALE + jnp.log2(total)
+        tag_far[pl.ds(ci * GROUPS, GROUPS)] = to_groups(lse)
+        low, high = to_lanes(lse)
         stat_far[ci, :, :128] = low
         stat_far[ci, :, 128:] = high
 
@@ -297,6 +324,11 @@
 
         @pl.when(i == 2)
         def _():
+            hear(2, count_z(4))
+            for device in along_x():
+                tell(3, device)
+            hear(3, 3)
+            pl.when(is_late)(functools.partial(tell, 4, partner))
             k_wait(w_left)
             k_copy(w_left, 3, w_right).start()
             k_copy(w_left, 4, w_core).start()
@@ -323,6 +355,7 @@
             v_copy(far_block, 6, w_core).start()
             k_wait(place(2, 1))
             v_wait(place(2, 1))
+            pl.when(is_early)(functools.partial(hear, 4, 1))
 
         @pl.when(jnp.logical_and(is_early, i >= 5))
         def _():
@@ -334,7 +367,7 @@
 
         @pl.when(jnp.logical_and(i < 8, block < w))
         def _():
-            triangle(block, False)
+            triangle(block, False, range(ROWS // TILE))
 
         @pl.when(i == 7)
         def _():
@@ -396,12 +429,31 @@
     lax.fori_loop(1, HALF, col_start, 0)
     column_in[w] = column_out[w]
 
-    def arrived(j, carry):
-        hg = lax.rem(h + j, HEADS)
-        copy(send_own.at[hg], got_own.at[hg], own_send.at[hg], own_recv.at[hg], (hg, b)).wait_recv()
-        return carry
-
-    lax.fori_loop(1, HEADS, arrived, 0)
+    others, everyone = pl.ds(0, HEADS - 1), pl.ds(0, HEADS)
+
+    def all_own(which):
+        return copy(
+            send_own.at[which], got_own.at[which], own_send.at[0], own_recv.at[0], half_device(w_core)
+        )
+
+    def all_own_stat(which):
+        return copy(
+            tag_own.at[which], got_stat_own.at[which],
+            own_stat_send.at[0], own_stat_recv.at[0], half_device(w_core),
+        )
+
+    def all_far(which):
+        return copy(
+            send_far.at[which], got_far.at[which], far_send.at[0], far_recv.at[0], partner
+        )
+
+    def all_far_stat(which):
+        return copy(
+            tag_far.at[which], got_stat_far.at[which],
+            far_stat_send.at[0], far_stat_recv.at[0], partner,
+        )
+
+    all_own(others).wait_recv()
 
     @pl.when(is_early)
     def _():
@@ -410,32 +462,14 @@
 
     @pl.when(is_late)
     def _():
-        def stat_arrived(j, carry):
-            hg = lax.rem(h + j, HEADS)
-            copy(
-                stat_own.at[0], got_stat_own.at[hg], own_stat_send.at[hg], own_stat_recv.at[hg], (hg, b)
-            ).wait_recv()
-            return carry
-
-        lax.fori_loop(1, HEADS, stat_arrived, 0)
-
-        def far_arrived(j, carry):
-            hg = lax.rem(h + j, HEADS)
-            device = (hg, w)
-            copy(send_far.at[hg], got_far.at[hg], far_send.at[hg], far_recv.at[hg], device).wait_recv()
-            copy(
-                stat_far.at[0], got_stat_far.at[hg], far_stat_send.at[hg], far_stat_recv.at[hg], device
-            ).wait_recv()
-            return carry
-
-        lax.fori_loop(0, HEADS, far_arrived, 0)
-        pad = jnp.zeros((128 - HEADS, 256), jnp.float32)
+        all_own_stat(others).wait_recv()
+        all_far(everyone).wait_recv()
+        all_far_stat(everyone).wait_recv()
+        pad = jnp.zeros((128 - HEADS, 128), jnp.float32)
         stat_a = jnp.concatenate([got_stat_own[hh] for hh in range(HEADS)] + [pad], axis=0)
         stat_b = jnp.concatenate([got_stat_far[hh] for hh in range(HEADS)] + [pad], axis=0)
-        turned_a[...] = jnp.transpose(stat_a)
-        turned_b[...] = jnp.transpose(stat_b)
-        mine = pl.ds(pl.multiple_of(z * GROUP, 8), GROUP)
-        lse_a, lse_b = turned_a[mine, :], turned_b[mine, :]
+        lse_a = jnp.transpose(stat_a)[:GROUP]
+        lse_b = jnp.transpose(stat_b)[:GROUP]
         share_a = 1.0 / (1.0 + jnp.exp2(lse_b - lse_a))
         share_b = 1.0 / (1.0 + jnp.exp2(lse_a - lse_b))
         for hh in range(HEADS):
@@ -463,26 +497,16 @@
         k_copy(w, slot, w_core).wait_send()
         v_copy(w, slot, w_core).wait_send()
 
-    def own_left(j, carry):
-        hg = lax.rem(h + j, HEADS)
-        own_copy(hg).wait_send()
-
-        @pl.when(is_late)
-        def _():
-            own_stat_copy(hg).wait_send()
-
-        return carry
-
-    lax.fori_loop(1, HEADS, own_left, 0)
+    all_own(others).wait_send()
+
+    @pl.when(is_late)
+    def _():
+        all_own_stat(others).wait_send()
 
     @pl.when(is_early)
     def _():
-        def far_left(hg, carry):
-            far_copy(hg).wait_send()
-            far_stat_copy(hg).wait_send()
-            return carry
-
-        lax.fori_loop(0, HEADS, far_left, 0)
+        all_far(everyone).wait_send()
+        all_far_stat(everyone).wait_send()
 
     def chunk_left(ci, carry):
         peer_copy(stat_own, ci).wait_send()
@@ -533,19 +557,20 @@
             vmem((CHUNKS, 1, 256), f32),
             vmem((CHUNKS, 1, 256), f32),
             vmem((CHUNKS, 1, 256), f32),
+            vmem((HEADS, 1, 128), f32),
+            vmem((HEADS, 1, 128), f32),
             vmem((HEADS, GROUP, DIM), bf16),
             vmem((HEADS, GROUP, DIM), bf16),
-            vmem((HEADS, 1, 256), f32),
-            vmem((HEADS, 1, 256), f32),
-            vmem((256, 128), f32),
-            vmem((256, 128), f32),
+            vmem((HEADS, 1, 128), f32),
+            vmem((HEADS, 1, 128), f32),
             vmem((HALF, 8, ROWS), f32),
             vmem((HALF, 1, ROWS), f32),
             vmem((HALF, 1, ROWS), f32),
             dma((7,)), dma((HALF,)), dma((7,)), dma((HALF,)), dma((CHUNKS,)), dma((CHUNKS,)),
-            dma((HEADS,)), dma((HEADS,)), dma((HEADS,)), dma((HEADS,)),
-            dma((HEADS,)), dma((HEADS,)), dma((HEADS,)), dma((HEADS,)),
+            dma((1,)), dma((1,)), dma((1,)), dma((1,)),
+            dma((1,)), dma((1,)), dma((1,)), dma((1,)),
             dma((CHUNKS,)), dma((CHUNKS,)), dma((HALF,)), dma((HALF,)),
+            pltpu.SemaphoreType.REGULAR((5,)),
         ],
         compiler_params=pltpu.CompilerParams(
             collective_id=0, has_side_effects=True, vmem_limit_bytes=58 * 1024 * 1024

time: 72.1 us -> 65.4 us (0.907)
  the two profiles are of different devices: /device:TPU:1 before, /device:TPU:33 now
where the time goes in v2:
time: 65.4 us; the launch traced here: 65.3 us
  Pallas kernels  62.4 us (95%)
  local copies, waits for them, and re-layouts  2.2 us (3%)
    pallas_call x1, Pallas kernels, local(): pl.pallas_call(kernel, out_shape=(jax.ShapeDtypeStruct((GROUP, HEADS * DI...  62.4 us
    unnamed x4, local copies, waits for them, and re-layouts  2.2 us

profile of v2, /device:TPU:33, one launch (start us, length us, event | category | flops | bytes accessed | tf_op | source)
XLA Modules:
  0.0 65.3 jit_solution(1955722563301268487)
XLA Ops:
  0.6 62.4 %shard_map.50 = (bf16[24,4096]{1,0:T(8,128)(2,1)}, f32[1,768]{1,0:T(1,128)}) custom-call(bf16[768,128]{1,0:T(8,128)(2,1)} %q_ref.1, bf16[768,128]{1,0:T(8,128)(2,1)} %k_ref.1, bf16[768,128]{1,0:T(8,128)(2,1)} %v_ref.1), custom_call_target="tpu_custom_call" | custom-call | tf_op jit(solution)/shard_map/pallas_call | solution.py:534
  63.1 0.0 copy-start
  63.1 1.6 %copy.7 = bf16[24,4096]{1,0:T(8,128)(2,1)} copy(bf16[24,4096]{1,0:T(8,128)(2,1)} %get-tuple-element.4) | data formatting | bytes 393216
  64.7 0.0 copy-done
  64.7 0.6 copy.8
Async XLA Ops:
  63.1 1.6 %copy-start = (f32[1,768]{1,0:T(1,128)S(1)}, f32[1,768]{1,0:T(1,128)}, u32[]{:S(2)}) copy-start(f32[1,768]{1,0:T(1,128)} %get-tuple-element.5) | copy-start | bytes 9220

commit v3 on v2

--- a/solution.py
+++ b/solution.py
@@ -163,13 +163,10 @@
         rows = pl.ds(pl.multiple_of(ci * CHUNK, CHUNK), CHUNK)
         return copy(q_ref.at[rows], q_far.at[rows], q_send.at[ci], q_recv.at[ci], partner)
 
-    @pl.when(is_late)
-    def _():
-        def start(i, carry):
-            q_copy(lax.rem(x + i, CHUNKS)).start()
-            return carry
-
-        lax.fori_loop(0, CHUNKS, start, 0)
+    def send_queries(i):
+        pl.when(is_late)(lambda: q_copy(lax.rem(x + i, CHUNKS)).start())
+
+    send_queries(0)
 
     def k_copy(block, slot, to):
         return copy(keys.at[block], keys.at[block], k_send.at[slot], k_recv.at[block], half_device(to))
@@ -191,6 +188,7 @@
     triangle(w, True, (1,))
     hear(1, count_z(2))
     tell_z(2, 4)
+    send_queries(1)
     column[...] = jnp.zeros_like(column)
 
     def k_wait(block):
@@ -272,7 +270,7 @@
         def _():
             got_stat_own[h] = tag_own[h]
 
-    def rectangle(ci):
+    def rectangle(ci, first):
         q_copy(ci).wait_recv()
         rows = pl.ds(pl.multiple_of(ci * CHUNK, CHUNK), CHUNK)
         local = pl.ds(0, CHUNK)
@@ -307,6 +305,8 @@
         stat_far[ci, :, :128] = low
         stat_far[ci, :, 128:] = high
 
+        pl.when(first)(functools.partial(hear, 4, 1))
+
         def start(g, carry):
             hg = ci * GROUPS + lax.rem(z + g, GROUPS)
             far_copy(hg).start()
@@ -329,6 +329,7 @@
                 tell(3, device)
             hear(3, 3)
             pl.when(is_late)(functools.partial(tell, 4, partner))
+            send_queries(2)
             k_wait(w_left)
             k_copy(w_left, 3, w_right).start()
             k_copy(w_left, 4, w_core).start()
@@ -342,11 +343,12 @@
 
         @pl.when(i == 4)
         def _():
+            send_queries(3)
             for dy in (3, 1):
                 k_wait(place(dy, 1))
                 v_wait(place(dy, 1))
 
-        @pl.when(i == 5)
+        @pl.when(i == 6)
         def _():
             far_block = place(2, 0)
             k_wait(far_block)
@@ -355,27 +357,33 @@
             v_copy(far_block, 6, w_core).start()
             k_wait(place(2, 1))
             v_wait(place(2, 1))
-            pl.when(is_early)(functools.partial(hear, 4, 1))
-
-        @pl.when(jnp.logical_and(is_early, i >= 5))
-        def _():
-            rectangle(lax.rem(x + i - 5, CHUNKS))
-
-        dy = jnp.where(i == 1, 0, jnp.where(i >= 6, 2, jnp.where(lax.rem(i, 2) == 0, 3, 1)))
-        flip = jnp.where(jnp.logical_or(i == 1, jnp.logical_or(i == 4, jnp.logical_or(i == 5, i == 7))), 1, 0)
-        block = place(dy, flip)
-
-        @pl.when(jnp.logical_and(i < 8, block < w))
-        def _():
-            triangle(block, False, range(ROWS // TILE))
-
-        @pl.when(i == 7)
+
+        @pl.when(jnp.logical_and(is_early, i >= 6))
+        def _():
+            rectangle(lax.rem(x + i - 6, CHUNKS), i == 6)
+
+        def unit(u, carry):
+            dy = jnp.where(u == 1, 0, jnp.where(u >= 6, 2, jnp.where(lax.rem(u, 2) == 0, 3, 1)))
+            flip = jnp.where(jnp.logical_or(u == 1, jnp.logical_or(u == 4, jnp.logical_or(u == 5, u == 7))), 1, 0)
+            block = place(dy, flip)
+
+            @pl.when(block < w)
+            def _():
+                triangle(block, False, range(ROWS // TILE))
+
+            return carry
+
+        first = jnp.where(i <= 5, i, 6)
+        last = jnp.where(i <= 5, i + 1, jnp.where(i == 8, 8, 6))
+        lax.fori_loop(first, last, unit, 0)
+
+        @pl.when(i == 8)
         def _():
             settle_triangle()
 
         return carry
 
-    lax.fori_loop(1, 9, step, 0)
+    lax.fori_loop(1, 10, step, 0)
 
     def add_columns(count, rows, tops, weights, lse, width):
         per = width // ROWS
@@ -395,25 +403,39 @@
         top = jnp.maximum(one, two)
         return top + jnp.log2(jnp.exp2(one - top) + jnp.exp2(two - top))
 
-    def columns(i, carry):
+    def piece(i):
         ci = lax.rem(x + i, CHUNKS)
-        rows = pl.ds(pl.multiple_of(ci * CHUNK, CHUNK), CHUNK)
-        peer_copy(stat_own, ci).wait_recv()
-
-        @pl.when(is_early)
-        def _():
+        return ci, pl.ds(pl.multiple_of(ci * CHUNK, CHUNK), CHUNK)
+
+    @pl.when(is_early)
+    def _():
+        def near(i, carry):
+            ci, rows = piece(i)
             add_columns(w + 1, rows, top_tri, weights_tri, lse_col[rows, :], ROWS)
+            return carry
+
+        lax.fori_loop(0, CHUNKS, near, 0)
+
+        def distant(i, carry):
+            ci, rows = piece(i)
+            peer_copy(stat_own, ci).wait_recv()
             lse = to_column(both(stat_far[ci], stat_peer[ci]))
             add_columns(HALF // 2, rows, top_far, weights_far, lse, WIDE)
-
-        @pl.when(is_late)
-        def _():
+            return carry
+
+        lax.fori_loop(0, CHUNKS, distant, 0)
+
+    @pl.when(is_late)
+    def _():
+        def near(i, carry):
+            ci, rows = piece(i)
+            peer_copy(stat_own, ci).wait_recv()
             lse = to_column(both(stat_own[ci], stat_peer[ci]))
             add_columns(w + 1, rows, top_tri, weights_tri, lse, ROWS)
-
-        return carry
-
-    lax.fori_loop(0, CHUNKS, columns, 0)
+            return carry
+
+        lax.fori_loop(0, CHUNKS, near, 0)
+
     for j in range(HALF):
         column_out[j] = jnp.sum(column[j], axis=0, keepdims=True)
 

time: 65.4 us -> 58.6 us (0.90)
  Pallas kernels: 62.4 us -> 55.6 us
    pallas_call x1, Pallas kernels: 62.4 us -> 55.6 us  [local(): pl.pallas_call(kernel, out_shape=(jax.ShapeDtypeStruct((GROUP, HEADS * DI...]
where the time goes in v3:
time: 58.6 us; the launch traced here: 58.5 us
  Pallas kernels  55.6 us (95%)
  local copies, waits for them, and re-layouts  2.2 us (4%)
  between operations  0.65 us (1%)
    pallas_call x1, Pallas kernels, local(): pl.pallas_call(kernel, out_shape=(jax.ShapeDtypeStruct((GROUP, HEADS * DI...  55.6 us
    unnamed x4, local copies, waits for them, and re-layouts  2.2 us

profile of v3, /device:TPU:33, one launch (start us, length us, event | category | flops | bytes accessed | tf_op | source)
XLA Modules:
  0.0 58.5 jit_solution(13860260697010640604)
XLA Ops:
  0.6 55.6 %shard_map.50 = (bf16[24,4096]{1,0:T(8,128)(2,1)}, f32[1,768]{1,0:T(1,128)}) custom-call(bf16[768,128]{1,0:T(8,128)(2,1)} %q_ref.1, bf16[768,128]{1,0:T(8,128)(2,1)} %k_ref.1, bf16[768,128]{1,0:T(8,128)(2,1)} %v_ref.1), custom_call_target="tpu_custom_call" | custom-call | tf_op jit(solution)/shard_map/pallas_call | solution.py:556
  56.3 0.0 copy-start
  56.3 1.6 %copy.7 = bf16[24,4096]{1,0:T(8,128)(2,1)} copy(bf16[24,4096]{1,0:T(8,128)(2,1)} %get-tuple-element.4) | data formatting | bytes 393216
  57.9 0.0 copy-done
  57.9 0.6 copy.8
Async XLA Ops:
  56.3 1.6 %copy-start = (f32[1,768]{1,0:T(1,128)S(1)}, f32[1,768]{1,0:T(1,128)}, u32[]{:S(2)}) copy-start(f32[1,768]{1,0:T(1,128)} %get-tuple-element.5) | copy-start | bytes 9220

commit v4 on v3

--- a/solution.py
+++ b/solution.py
@@ -18,7 +18,9 @@
 GROUP = ROWS // HEADS
 GROUPS = CHUNK // GROUP
 TILE = 384
-WIDE = 1536
+WIDE = 3072
+PER = WIDE // ROWS
+TILES = HALF // PER
 SCALE = math.log2(math.e) / math.sqrt(DIM)
 LOW = -1e30
 
@@ -81,7 +83,7 @@
     k_send, k_recv, v_send, v_recv, q_send, q_recv,
     own_send, own_recv, own_stat_send, own_stat_recv,
     far_send, far_recv, far_stat_send, far_stat_recv,
-    peer_send, peer_recv, col_send, col_recv, ready,
+    peer_send, peer_recv, col_send, col_recv, ready, local_sem, q_own,
 ):
     h = lax.axis_index("head")
     b = lax.axis_index("blk")
@@ -140,13 +142,17 @@
     def hear(index, count):
         pl.semaphore_wait(ready.at[index], count)
 
-    keys[w] = k_ref[...]
-    values[w] = v_ref[...]
+    inside = [
+        pltpu.make_async_copy(src, dst, local_sem.at[n])
+        for n, (src, dst) in enumerate(((q_ref, q_own), (k_ref, keys.at[w]), (v_ref, values.at[w])))
+    ]
+    for one in inside:
+        one.start()
 
     def triangle(block, masked, tiles):
         for t in tiles:
             rows = pl.ds(t * TILE, TILE)
-            logits = dot_rows(q_ref[rows, :], keys[block])
+            logits = dot_rows(q_own[rows, :], keys[block])
             if masked:
                 row = lax.broadcasted_iota(jnp.int32, logits.shape, 0) + t * TILE
                 col = lax.broadcasted_iota(jnp.int32, logits.shape, 1)
@@ -174,14 +180,25 @@
     def v_copy(block, slot, to):
         return copy(values.at[block], values.at[block], v_send.at[slot], v_recv.at[block], half_device(to))
 
-    k_copy(w, 0, w_right).start()
-    k_copy(w, 1, w_left).start()
-    k_copy(w, 2, w_core).start()
-    v_copy(w, 0, w_right).start()
-    v_copy(w, 1, w_left).start()
-    v_copy(w, 2, w_core).start()
+    def own_copy_out(src, dst, send_sem, recv_sem, slot, to):
+        return copy(src, dst.at[w], send_sem.at[slot], recv_sem.at[w], half_device(to))
+
+    def k_out(slot, to):
+        own_copy_out(k_ref, keys, k_send, k_recv, slot, to).start()
+
+    def v_out(slot, to):
+        own_copy_out(v_ref, values, v_send, v_recv, slot, to).start()
+
+    k_out(0, w_right)
+    v_out(1, w_left)
+    k_out(2, w_core)
+    v_out(2, w_core)
+    v_out(0, w_right)
+    k_out(1, w_left)
 
     tell_z(0, 1)
+    for one in inside:
+        one.wait()
     triangle(w, True, (0,))
     hear(0, count_z(1))
     tell_z(1, 2)
@@ -276,8 +293,9 @@
         local = pl.ds(0, CHUNK)
 
         def step(d, carry):
-            key_tile = keys[pl.ds(d * 2, 2)].reshape(WIDE, DIM)
-            value_tile = values[pl.ds(d * 2, 2)].reshape(WIDE, DIM)
+            blocks = pl.ds(d * PER, PER)
+            key_tile = keys[blocks].reshape(WIDE, DIM)
+            value_tile = values[blocks].reshape(WIDE, DIM)
             logits = dot_rows(q_far[rows, :], key_tile)
             top, total, weights, out = weigh(logits, value_tile)
             weights_far[d, rows, :] = weights
@@ -286,13 +304,14 @@
             out_far[d, local, :] = out
             return carry
 
-        lax.fori_loop(0, HALF // 2, step, 0, unroll=2)
+        for d in range(TILES):
+            step(d, 0)
         top = top_far[0, rows, :]
-        for d in range(1, HALF // 2):
+        for d in range(1, TILES):
             top = jnp.maximum(top, top_far[d, rows, :])
         total = jnp.zeros((CHUNK, 128), jnp.float32)
         out = jnp.zeros((CHUNK, 128), jnp.float32)
-        for d in range(HALF // 2):
+        for d in range(TILES):
             factor = jnp.exp2((top_far[d, rows, :] - top) * SCALE)
             total = total + factor * total_far[d]
             out = out + factor * out_far[d]
@@ -333,13 +352,13 @@
             k_wait(w_left)
             k_copy(w_left, 3, w_right).start()
             k_copy(w_left, 4, w_core).start()
-            k_wait(w_right)
-            k_copy(w_right, 5, w_core).start()
             v_wait(w_right)
             v_copy(w_right, 3, w_left).start()
             v_copy(w_right, 5, w_core).start()
             v_wait(w_left)
             v_copy(w_left, 4, w_core).start()
+            k_wait(w_right)
+            k_copy(w_right, 5, w_core).start()
 
         @pl.when(i == 4)
         def _():
@@ -358,9 +377,9 @@
             k_wait(place(2, 1))
             v_wait(place(2, 1))
 
-        @pl.when(jnp.logical_and(is_early, i >= 6))
-        def _():
-            rectangle(lax.rem(x + i - 6, CHUNKS), i == 6)
+        @pl.when(jnp.logical_and(is_early, jnp.logical_and(i >= 6, i != 8)))
+        def _():
+            rectangle(lax.rem(x + jnp.where(i < 8, i - 6, i - 7), CHUNKS), i == 6)
 
         def unit(u, carry):
             dy = jnp.where(u == 1, 0, jnp.where(u >= 6, 2, jnp.where(lax.rem(u, 2) == 0, 3, 1)))
@@ -377,13 +396,13 @@
         last = jnp.where(i <= 5, i + 1, jnp.where(i == 8, 8, 6))
         lax.fori_loop(first, last, unit, 0)
 
-        @pl.when(i == 8)
+        @pl.when(i == jnp.where(y <= 1, 5, 8))
         def _():
             settle_triangle()
 
         return carry
 
-    lax.fori_loop(1, 10, step, 0)
+    lax.fori_loop(1, 11, step, 0)
 
     def add_columns(count, rows, tops, weights, lse, width):
         per = width // ROWS
@@ -420,7 +439,7 @@
             ci, rows = piece(i)
             peer_copy(stat_own, ci).wait_recv()
             lse = to_column(both(stat_far[ci], stat_peer[ci]))
-            add_columns(HALF // 2, rows, top_far, weights_far, lse, WIDE)
+            add_columns(TILES, rows, top_far, weights_far, lse, WIDE)
             return carry
 
         lax.fori_loop(0, CHUNKS, distant, 0)
@@ -552,14 +571,13 @@
     bf16, f32 = jnp.bfloat16, jnp.float32
     vmem, dma = pltpu.VMEM, pltpu.SemaphoreType.DMA
     whole = pl.BlockSpec(memory_space=pltpu.VMEM)
-    quarter = HALF // 2
     return pl.pallas_call(
         kernel,
         out_shape=(
             jax.ShapeDtypeStruct((GROUP, HEADS * DIM), bf16),
             jax.ShapeDtypeStruct((1, ROWS), f32),
         ),
-        in_specs=[whole] * 3,
+        in_specs=[pl.BlockSpec(memory_space=pl.ANY)] * 3,
         out_specs=(whole, whole),
         scratch_shapes=[
             vmem((HALF, ROWS, DIM), bf16),
@@ -569,10 +587,10 @@
             vmem((HALF, ROWS, 128), f32),
             vmem((HALF, ROWS, 128), f32),
             vmem((HALF, ROWS, DIM), f32),
-            vmem((quarter, ROWS, WIDE), bf16),
-            vmem((quarter, ROWS, 128), f32),
-            vmem((quarter, CHUNK, 128), f32),
-            vmem((quarter, CHUNK, DIM), f32),
+            vmem((TILES, ROWS, WIDE), bf16),
+            vmem((TILES, ROWS, 128), f32),
+            vmem((TILES, CHUNK, 128), f32),
+            vmem((TILES, CHUNK, DIM), f32),
             vmem((ROWS, 128), f32),
             vmem((HEADS, GROUP, DIM), bf16),
             vmem((HEADS, GROUP, DIM), bf16),
@@ -593,6 +611,8 @@
             dma((1,)), dma((1,)), dma((1,)), dma((1,)),
             dma((CHUNKS,)), dma((CHUNKS,)), dma((HALF,)), dma((HALF,)),
             pltpu.SemaphoreType.REGULAR((5,)),
+            dma((3,)),
+            vmem((ROWS, DIM), bf16),
         ],
         compiler_params=pltpu.CompilerParams(
             collective_id=0, has_side_effects=True, vmem_limit_bytes=58 * 1024 * 1024

time: 58.6 us -> 56.1 us (0.957)
  the two profiles are of different devices: /device:TPU:33 before, /device:TPU:449 now
where the time goes in v4:
time: 56.1 us; the launch traced here: 56 us
  Pallas kernels  53.1 us (95%)
  local copies, waits for them, and re-layouts  2.2 us (4%)
  between operations  0.65 us (1%)
    pallas_call x1, Pallas kernels, local(): pl.pallas_call(kernel, out_shape=(jax.ShapeDtypeStruct((GROUP, HEADS * DI...  53.1 us
    unnamed x4, local copies, waits for them, and re-layouts  2.2 us

profile of v4, /device:TPU:449, one launch (start us, length us, event | category | flops | bytes accessed | tf_op | source)
XLA Modules:
  0.0 56.0 jit_solution(9045404371406662616)
XLA Ops:
  0.6 53.1 %shard_map.50 = (bf16[24,4096]{1,0:T(8,128)(2,1)}, f32[1,768]{1,0:T(1,128)}) custom-call(bf16[768,128]{1,0:T(8,128)(2,1)} %q_ref.1, bf16[768,128]{1,0:T(8,128)(2,1)} %k_ref.1, bf16[768,128]{1,0:T(8,128)(2,1)} %v_ref.1), custom_call_target="tpu_custom_call" | custom-call | tf_op jit(solution)/shard_map/pallas_call | solution.py:574
  53.8 0.0 copy-start
  53.8 1.6 %copy.7 = bf16[24,4096]{1,0:T(8,128)(2,1)} copy(bf16[24,4096]{1,0:T(8,128)(2,1)} %get-tuple-element.4) | data formatting | bytes 393216
  55.4 0.0 copy-done
  55.4 0.6 %copy.8 = f32[1,768]{1,0:T(1,128)} copy(f32[1,768]{1,0:T(1,128)S(1)} %copy-done) | data formatting | bytes 6144
Async XLA Ops:
  53.8 1.6 %copy-start = (f32[1,768]{1,0:T(1,128)S(1)}, f32[1,768]{1,0:T(1,128)}, u32[]{:S(2)}) copy-start(f32[1,768]{1,0:T(1,128)} %get-tuple-element.5) | copy-start | bytes 9220

commit v5 on v4

--- a/solution.py
+++ b/solution.py
@@ -214,6 +214,11 @@
     def v_wait(block):
         v_copy(block, 0, w_core).wait_recv()
 
+    k_wait(w_left)
+    k_copy(w_left, 3, w_right).start()
+    v_wait(w_right)
+    v_copy(w_right, 3, w_left).start()
+
     def own_copy(hg):
         return copy(send_own.at[hg], got_own.at[h], own_send.at[0], own_recv.at[0], (hg, b))
 
@@ -324,7 +329,7 @@
         stat_far[ci, :, :128] = low
         stat_far[ci, :, 128:] = high
 
-        pl.when(first)(functools.partial(hear, 4, 1))
+        pl.when(first)(functools.partial(hear, 3, 1))
 
         def start(g, carry):
             hg = ci * GROUPS + lax.rem(z + g, GROUPS)
@@ -338,23 +343,16 @@
     def step(i, carry):
         @pl.when(i == 1)
         def _():
+            hear(2, count_z(4))
+            pl.when(is_late)(functools.partial(tell, 3, partner))
             k_wait(w_core)
             v_wait(w_core)
 
         @pl.when(i == 2)
         def _():
-            hear(2, count_z(4))
-            for device in along_x():
-                tell(3, device)
-            hear(3, 3)
-            pl.when(is_late)(functools.partial(tell, 4, partner))
+            k_copy(w_left, 4, w_core).start()
+            v_copy(w_right, 5, w_core).start()
             send_queries(2)
-            k_wait(w_left)
-            k_copy(w_left, 3, w_right).start()
-            k_copy(w_left, 4, w_core).start()
-            v_wait(w_right)
-            v_copy(w_right, 3, w_left).start()
-            v_copy(w_right, 5, w_core).start()
             v_wait(w_left)
             v_copy(w_left, 4, w_core).start()
             k_wait(w_right)
@@ -377,9 +375,9 @@
             k_wait(place(2, 1))
             v_wait(place(2, 1))
 
-        @pl.when(jnp.logical_and(is_early, jnp.logical_and(i >= 6, i != 8)))
-        def _():
-            rectangle(lax.rem(x + jnp.where(i < 8, i - 6, i - 7), CHUNKS), i == 6)
+        @pl.when(jnp.logical_and(is_early, jnp.logical_and(i >= 6, i != 9)))
+        def _():
+            rectangle(lax.rem(x + jnp.where(i < 9, i - 6, i - 7), CHUNKS), i == 6)
 
         def unit(u, carry):
             dy = jnp.where(u == 1, 0, jnp.where(u >= 6, 2, jnp.where(lax.rem(u, 2) == 0, 3, 1)))
@@ -393,10 +391,10 @@
             return carry
 
         first = jnp.where(i <= 5, i, 6)
-        last = jnp.where(i <= 5, i + 1, jnp.where(i == 8, 8, 6))
+        last = jnp.where(i <= 5, i + 1, jnp.where(i == 9, 8, 6))
         lax.fori_loop(first, last, unit, 0)
 
-        @pl.when(i == jnp.where(y <= 1, 5, 8))
+        @pl.when(i == jnp.where(y <= 1, 5, 9))
         def _():
             settle_triangle()
 
@@ -567,11 +565,29 @@
     lax.fori_loop(1, HALF, col_left, 0)
 
 
+def hand_over_kernel(att_ref, heavy_ref, att_out, heavy_out):
+    att_out[...] = att_ref[...]
+    heavy_out[...] = heavy_ref[...]
+
+
+def hand_over(attended, heavy):
+    whole = pl.BlockSpec(memory_space=pltpu.VMEM)
+    return pl.pallas_call(
+        hand_over_kernel,
+        out_shape=(
+            jax.ShapeDtypeStruct(attended.shape, attended.dtype),
+            jax.ShapeDtypeStruct(heavy.shape, heavy.dtype),
+        ),
+        in_specs=[whole] * 2,
+        out_specs=(whole, whole),
+    )(attended, heavy)
+
+
 def local(queries, key_states, value_states):
     bf16, f32 = jnp.bfloat16, jnp.float32
     vmem, dma = pltpu.VMEM, pltpu.SemaphoreType.DMA
     whole = pl.BlockSpec(memory_space=pltpu.VMEM)
-    return pl.pallas_call(
+    attended, heavy = pl.pallas_call(
         kernel,
         out_shape=(
             jax.ShapeDtypeStruct((GROUP, HEADS * DIM), bf16),
@@ -610,7 +626,7 @@
             dma((1,)), dma((1,)), dma((1,)), dma((1,)),
             dma((1,)), dma((1,)), dma((1,)), dma((1,)),
             dma((CHUNKS,)), dma((CHUNKS,)), dma((HALF,)), dma((HALF,)),
-            pltpu.SemaphoreType.REGULAR((5,)),
+            pltpu.SemaphoreType.REGULAR((4,)),
             dma((3,)),
             vmem((ROWS, DIM), bf16),
         ],
@@ -618,6 +634,7 @@
             collective_id=0, has_side_effects=True, vmem_limit_bytes=58 * 1024 * 1024
         ),
     )(queries, key_states, value_states)
+    return hand_over(attended, heavy)
 
 
 def solution(mesh):

time: 56.1 us -> 55.3 us (0.986)
  the two profiles are of different devices: /device:TPU:449 before, /device:TPU:33 now
where the time goes in v5:
time: 55.3 us; the launch traced here: 55.1 us
  Pallas kernels  54.5 us (99%)
  between operations  0.64 us (1%)
    pallas_call x1, Pallas kernels, local(): pl.pallas_call(kernel, out_shape=(jax.ShapeDtypeStruct((GROUP, HEADS * DI...  52.9 us
    pallas_call x1, Pallas kernels, hand_over(): pl.pallas_call(hand_over_kernel, out_shape=(jax.ShapeDtypeStruct(attended...  1.62 us

profile of v5, /device:TPU:33, one launch (start us, length us, event | category | flops | bytes accessed | tf_op | source)
XLA Modules:
  0.0 55.1 jit_solution(13364887373201825373)
XLA Ops:
  0.6 52.9 %shard_map.50 = (bf16[24,4096]{1,0:T(8,128)(2,1)}, f32[1,768]{1,0:T(1,128)}) custom-call(bf16[768,128]{1,0:T(8,128)(2,1)} %q_ref.1, bf16[768,128]{1,0:T(8,128)(2,1)} %k_ref.1, bf16[768,128]{1,0:T(8,128)(2,1)} %v_ref.1), custom_call_target="tpu_custom_call" | custom-call | tf_op jit(solution)/shard_map/pallas_call | solution.py:590
  53.5 1.6 %shard_map.51 = (bf16[24,4096]{1,0:T(8,128)(2,1)}, f32[1,768]{1,0:T(1,128)}) custom-call(bf16[24,4096]{1,0:T(8,128)(2,1)} %get-tuple-element.4.att_ref, f32[1,768]{1,0:T(1,128)} %get-tuple-element.5.heavy_ref), custom_call_target="tpu_custom_call" | custom-call | tf_op jit(solution)/shard_map/pallas_call | solution.py:575

commit v6 on v5

--- a/solution.py
+++ b/solution.py
@@ -220,21 +220,21 @@
     v_copy(w_right, 3, w_left).start()
 
     def own_copy(hg):
-        return copy(send_own.at[hg], got_own.at[h], own_send.at[0], own_recv.at[0], (hg, b))
+        return copy(send_own.at[hg], got_own.at[h], own_send.at[hg], own_recv.at[h], (hg, b))
 
     def own_stat_copy(hg):
         return copy(
             tag_own.at[hg], got_stat_own.at[h],
-            own_stat_send.at[0], own_stat_recv.at[0], (hg, b),
+            own_stat_send.at[hg], own_stat_recv.at[h], (hg, b),
         )
 
     def far_copy(hg):
-        return copy(send_far.at[hg], got_far.at[h], far_send.at[0], far_recv.at[0], (hg, w + HALF))
+        return copy(send_far.at[hg], got_far.at[h], far_send.at[hg], far_recv.at[h], (hg, w + HALF))
 
     def far_stat_copy(hg):
         return copy(
             tag_far.at[hg], got_stat_far.at[h],
-            far_stat_send.at[0], far_stat_recv.at[0], (hg, w + HALF),
+            far_stat_send.at[hg], far_stat_recv.at[h], (hg, w + HALF),
         )
 
     def peer_copy(stat, ci):
@@ -468,31 +468,21 @@
     lax.fori_loop(1, HALF, col_start, 0)
     column_in[w] = column_out[w]
 
-    others, everyone = pl.ds(0, HEADS - 1), pl.ds(0, HEADS)
-
-    def all_own(which):
-        return copy(
-            send_own.at[which], got_own.at[which], own_send.at[0], own_recv.at[0], half_device(w_core)
-        )
-
-    def all_own_stat(which):
-        return copy(
-            tag_own.at[which], got_stat_own.at[which],
-            own_stat_send.at[0], own_stat_recv.at[0], half_device(w_core),
-        )
-
-    def all_far(which):
-        return copy(
-            send_far.at[which], got_far.at[which], far_send.at[0], far_recv.at[0], partner
-        )
-
-    def all_far_stat(which):
-        return copy(
-            tag_far.at[which], got_stat_far.at[which],
-            far_stat_send.at[0], far_stat_recv.at[0], partner,
-        )
-
-    all_own(others).wait_recv()
+    def each(begin, wait):
+        def one(j, carry):
+            wait(lax.rem(h + j, HEADS))
+            return carry
+
+        lax.fori_loop(begin, HEADS, one, 0)
+
+    def arrival(src, dst, send_sem, recv_sem, device):
+        def wait(hg):
+            copy(src.at[hg], dst.at[hg], send_sem.at[hg], recv_sem.at[hg], device).wait_recv()
+
+        return wait
+
+    near_by = half_device(w_core)
+    each(1, arrival(send_own, got_own, own_send, own_recv, near_by))
 
     @pl.when(is_early)
     def _():
@@ -501,9 +491,9 @@
 
     @pl.when(is_late)
     def _():
-        all_own_stat(others).wait_recv()
-        all_far(everyone).wait_recv()
-        all_far_stat(everyone).wait_recv()
+        each(1, arrival(tag_own, got_stat_own, own_stat_send, own_stat_recv, near_by))
+        each(0, arrival(send_far, got_far, far_send, far_recv, partner))
+        each(0, arrival(tag_far, got_stat_far, far_stat_send, far_stat_recv, partner))
         pad = jnp.zeros((128 - HEADS, 128), jnp.float32)
         stat_a = jnp.concatenate([got_stat_own[hh] for hh in range(HEADS)] + [pad], axis=0)
         stat_b = jnp.concatenate([got_stat_far[hh] for hh in range(HEADS)] + [pad], axis=0)
@@ -536,16 +526,16 @@
         k_copy(w, slot, w_core).wait_send()
         v_copy(w, slot, w_core).wait_send()
 
-    all_own(others).wait_send()
+    each(1, lambda hg: own_copy(hg).wait_send())
 
     @pl.when(is_late)
     def _():
-        all_own_stat(others).wait_send()
+        each(1, lambda hg: own_stat_copy(hg).wait_send())
 
     @pl.when(is_early)
     def _():
-        all_far(everyone).wait_send()
-        all_far_stat(everyone).wait_send()
+        each(0, lambda hg: far_copy(hg).wait_send())
+        each(0, lambda hg: far_stat_copy(hg).wait_send())
 
     def chunk_left(ci, carry):
         peer_copy(stat_own, ci).wait_send()
@@ -623,8 +613,8 @@
             vmem((HALF, 1, ROWS), f32),
             vmem((HALF, 1, ROWS), f32),
             dma((7,)), dma((HALF,)), dma((7,)), dma((HALF,)), dma((CHUNKS,)), dma((CHUNKS,)),
-            dma((1,)), dma((1,)), dma((1,)), dma((1,)),
-            dma((1,)), dma((1,)), dma((1,)), dma((1,)),
+            dma((HEADS,)), dma((HEADS,)), dma((HEADS,)), dma((HEADS,)),
+            dma((HEADS,)), dma((HEADS,)), dma((HEADS,)), dma((HEADS,)),
             dma((CHUNKS,)), dma((CHUNKS,)), dma((HALF,)), dma((HALF,)),
             pltpu.SemaphoreType.REGULAR((4,)),
             dma((3,)),

time: 55.3 us -> 58.7 us (1.061)
  Pallas kernels: 54.5 us -> 57.9 us
    pallas_call x1, Pallas kernels: 52.9 us -> 56.3 us  [local(): pl.pallas_call(kernel, out_shape=(jax.ShapeDtypeStruct((GROUP, HEADS * DI...]
where the time goes in v6:
time: 58.7 us; the launch traced here: 58.6 us
  Pallas kernels  57.9 us (99%)
  between operations  0.64 us (1%)
    pallas_call x1, Pallas kernels, local(): pl.pallas_call(kernel, out_shape=(jax.ShapeDtypeStruct((GROUP, HEADS * DI...  56.3 us
    pallas_call x1, Pallas kernels, hand_over(): pl.pallas_call(hand_over_kernel, out_shape=(jax.ShapeDtypeStruct(attended...  1.62 us

profile of v6, /device:TPU:33, one launch (start us, length us, event | category | flops | bytes accessed | tf_op | source)
XLA Modules:
  0.0 58.6 jit_solution(6092870956579466148)
XLA Ops:
  0.6 56.3 %shard_map.50 = (bf16[24,4096]{1,0:T(8,128)(2,1)}, f32[1,768]{1,0:T(1,128)}) custom-call(bf16[768,128]{1,0:T(8,128)(2,1)} %q_ref.1, bf16[768,128]{1,0:T(8,128)(2,1)} %k_ref.1, bf16[768,128]{1,0:T(8,128)(2,1)} %v_ref.1), custom_call_target="tpu_custom_call" | custom-call | tf_op jit(solution)/shard_map/pallas_call | solution.py:580
  56.9 1.6 %shard_map.51 = (bf16[24,4096]{1,0:T(8,128)(2,1)}, f32[1,768]{1,0:T(1,128)}) custom-call(bf16[24,4096]{1,0:T(8,128)(2,1)} %get-tuple-element.4.att_ref, f32[1,768]{1,0:T(1,128)} %get-tuple-element.5.heavy_ref), custom_call_target="tpu_custom_call" | custom-call | tf_op jit(solution)/shard_map/pallas_call | solution.py:565
